TPU v7x, 32 devices: a whole 2x2x4 slice. The times are simulated.
32 devices in a mesh: dp: 8 (over z, y), fsdp: 4 (over x, core).
Axes of the slice: x: 2, y: 2, z: 4, core: 2. Of those that a mesh axis runs over, the one named last changes fastest.
Arguments:
- inputs: bfloat16 [16, 1024, 1024], P('dp', 'fsdp'), may hold values from -6 to 6
- timestep: int32 [16], P('dp'), may hold values from 0 to 4999, as said below
- bucket_count: int32 [8], replicated, may hold values from 1 to 2, as said below
- upstream: bfloat16 [16, 1024, 1024], P('dp', 'fsdp'), may hold values from -6 to 6
- query_weight: bfloat16 [1024, 1024], P('fsdp'), may hold values from -0.1875 to 0.1875
- key_weight: bfloat16 [1024, 1024], P('fsdp'), may hold values from -0.1875 to 0.1875
- value_weight: bfloat16 [1024, 1024], P('fsdp'), may hold values from -0.1875 to 0.1875
- output_weight: bfloat16 [1024, 1024], P('fsdp'), may hold values from -1 to 1
- up_weight: bfloat16 [1024, 4096], P('fsdp'), may hold values from -0.1875 to 0.1875
- down_weight: bfloat16 [4096, 1024], P('fsdp'), may hold values from -0.09375 to 0.09375
- query_bias: bfloat16 [1024], P('fsdp'), may hold values from -2 to 2
- value_bias: bfloat16 [1024], P('fsdp'), may hold values from -2 to 2
- output_bias: bfloat16 [1024], P('fsdp'), may hold values from -2 to 2
- up_bias: bfloat16 [4096], P('fsdp'), may hold values from -2 to 2
- down_bias: bfloat16 [1024], P('fsdp'), may hold values from -2 to 2
- first_gain: bfloat16 [1024], P('fsdp'), may hold values from 0.5 to 1.5
- first_shift: bfloat16 [1024], P('fsdp'), may hold values from -2 to 2
- second_gain: bfloat16 [1024], P('fsdp'), may hold values from 0.5 to 1.5
- second_shift: bfloat16 [1024], P('fsdp'), may hold values from -2 to 2
Outputs:
- activations: bfloat16 [16, 1024, 1024], P('dp', 'fsdp')
- input_gradient: float32 [16, 1024, 1024], P('dp', 'fsdp')
- time_gradient: float32 [16, 1024], P('dp', 'fsdp')
- query_weight_gradient: float32 [1024, 1024], P('fsdp')
- key_weight_gradient: float32 [1024, 1024], P('fsdp')
- value_weight_gradient: float32 [1024, 1024], P('fsdp')
- output_weight_gradient: float32 [1024, 1024], P('fsdp')
- up_weight_gradient: float32 [1024, 4096], P('fsdp')
- down_weight_gradient: float32 [4096, 1024], P('fsdp')
- query_bias_gradient: float32 [1024], P('fsdp')
- value_bias_gradient: float32 [1024], P('fsdp')
- output_bias_gradient: float32 [1024], P('fsdp')
- up_bias_gradient: float32 [4096], P('fsdp')
- down_bias_gradient: float32 [1024], P('fsdp')
- first_gain_gradient: float32 [1024], P('fsdp')
- first_shift_gradient: float32 [1024], P('fsdp')
- second_gain_gradient: float32 [1024], P('fsdp')
- second_shift_gradient: float32 [1024], P('fsdp')
Inputs may be any that keep to these rules, and one draw needn't show every extreme that they name: Slots 0 to bucket_count[b] - 1 of bucket b are live, the others carry no gradient; the last bucket is always full. The timestep of sequence s lies in [b W, (b + 1) W) with b = s // 2 and W = 5000 divided by the number of buckets, rounded down.
All inputs are finite; a program needn't handle non-finite values.
Results may differ from a plain program's by a relative error of at most 0.017.
Values may be sent and summed in bfloat16 or wider, within the bound.
No kernel may reach another device: no remote copies, remote signals or barrier semaphores. Data moves between devices by JAX's collectives and lax.ppermute only.
A program may use at most 256 MiB of HBM per device.

v0:
```python
import functools
import math

import jax
import jax.numpy as jnp
from jax import lax
from jax.experimental import pallas as pl
from jax.experimental.pallas import tpu as pltpu
from jax.sharding import PartitionSpec as P

D = 1024
HEAD_DIM = 64
GROUP = 256
GROUP_HEADS = GROUP // HEAD_DIM
F32 = jnp.float32
BF16 = jnp.bfloat16
ROWS_ROWS = (((0,), (0,)), ((), ()))
COLS_COLS = (((1,), (1,)), ((), ()))
ANY = pl.BlockSpec(memory_space=pl.ANY)
VMEM_MB = dict(grad_z=16,grad_add=16,grad_join=16,lines_add=16,lines=16,relay=16,pair=16,two=16,grad_out=16,grad_y=24)
COST = 10**11
MICROSECONDS = dict(
    pick=2, cut=2, pack=3, split=2, copy=2, relay=2, columns=2, remote=3, key_value=7, query=4, attend=9, output=6,
    feed_forward=40, two=2, grad_x=8, grad_y=5, grad_z=3, grad_add=2, grad_join=3,
    grad_out=3, attend_back=15, delta=5, input=8, input_query=5, lines_in=2, lines=2, lines_add=1, pair=3,
)


def run_kernel(place, name, body, grid, ins, outs, later_than=(), scratch=(), aliases=None, vmem=16):
    count, waits = len(ins), len(later_than)

    def kernel(*refs):
        body(*refs[: 1 + count], *refs[1 + count + waits :])

    def spec(block, index, *buffers):
        if block is None:
            return ANY
        modes = dict(pipeline_mode=pl.Buffered(buffers[0])) if buffers else {}
        return pl.BlockSpec(block, index, **modes)

    shapes = [jax.ShapeDtypeStruct(shape, dtype) for shape, dtype, _, _ in outs]
    out_specs = [spec(block, index) for _, _, block, index in outs]
    single = len(outs) == 1
    return pl.pallas_call(
        kernel,
        grid_spec=pltpu.PrefetchScalarGridSpec(
            num_scalar_prefetch=1,
            grid=grid,
            in_specs=[spec(*one[1:]) for one in ins] + [ANY] * waits,
            out_specs=out_specs[0] if single else out_specs,
            scratch_shapes=list(scratch),
        ),
        out_shape=shapes[0] if single else shapes,
        input_output_aliases={1 + i: o for i, o in (aliases or {}).items()},
        compiler_params=pltpu.CompilerParams(vmem_limit_bytes=VMEM_MB.get(name, 60) * 2**20),
        cost_estimate=pl.CostEstimate(flops=int(MICROSECONDS[name] * COST), bytes_accessed=0, transcendentals=0),
        name=name,
    )(place, *[one[0] for one in ins], *later_than)


CHIP, CORE, SIDE_Y, SIDE_Z = range(4)
LINES = 16
QUERY_BIAS, VALUE_BIAS, OUTPUT_BIAS, DOWN_BIAS, GAIN1, SHIFT1, GAIN2, SHIFT2, EMBED, WEIGHT = range(10)


def device_of(at):
    return 2 * at[CHIP] + at[CORE]


def their(flip, at):
    return 2 * (at[CHIP] ^ flip) + (at[CORE] ^ 1)


def line(lines_ref, i):
    return lines_ref[i : i + 1, :]


def whole(array):
    return (array, array.shape, lambda *_: (0,) * array.ndim)


def held(array):
    return (*whole(array), 1)


def whole_out(shape, dtype):
    return (shape, dtype, shape, lambda *_: (0,) * len(shape))


def sinusoid(timestep):
    halves = D // 2
    frequency = jnp.exp(jnp.arange(halves, dtype=F32) * (-math.log(10000.0) / halves))
    angles = timestep.astype(F32)[:, None] * frequency[None, :]
    return jnp.concatenate([jnp.sin(angles), jnp.cos(angles)], axis=1)


def dot(left, right):
    return jnp.dot(left, right, preferred_element_type=F32)


def dot_back(left, right):
    return lax.dot_general(left, right, COLS_COLS, preferred_element_type=F32)


def outer(left, right):
    return lax.dot_general(left, right, ROWS_ROWS, preferred_element_type=F32)


def total(rows):
    return jnp.sum(rows, axis=0, keepdims=True)


def mean(rows):
    return jnp.mean(rows, axis=-1, keepdims=True)


def normalise(residual):
    centered = residual - mean(residual)
    scale = lax.rsqrt(mean(centered * centered) + 1e-05)
    return centered * scale, scale


def normalise_back(unit, scale, gain, grad):
    scaled = grad * gain
    return scale * (scaled - mean(scaled) - unit * mean(scaled * unit))


def gelu_and_slope(upward):
    size = jnp.abs(upward) * (2.0**-0.5)
    bell = jnp.exp(-0.5 * (upward * upward))
    t = 1.0 / (1.0 + 0.3275911 * size)
    series = t * (
        0.254829592
        + t * (-0.284496736 + t * (1.421413741 + t * (-1.453152027 + t * 1.061405429)))
    )
    tail = 0.5 * series * bell
    cdf = jnp.where(upward >= 0, 1.0 - tail, tail)
    return upward * cdf, cdf + upward * (bell * (2 * math.pi) ** -0.5)


def order_rows(at, pieces, weight_ref):
    for flip, piece in zip((0, 2, 1, 3), pieces):
        rows = piece.shape[0]
        start = pl.multiple_of((device_of(at) ^ flip) * rows, 16)
        weight_ref[pl.ds(start, rows), :] = piece[...]
    return weight_ref[...]


def pieces_in(pieces, step, firsts):
    return [(piece, (piece.shape[0], step), lambda j, *_, k=k: (0, k + j)) for piece, k in zip(pieces, firsts)]


def lines_in_kernel(at, own_ref, far_ref, embeds_ref, weight_ref, lines_ref, up_ref):
    share = D // 4
    extra = up_ref.shape[1] // D
    for flip, shares_ref, first in ((0, own_ref, 0), (2, own_ref, 16), (1, far_ref, 0), (3, far_ref, 16)):
        device = device_of(at) ^ flip
        rows = shares_ref[first : first + 16, :].astype(F32)
        piece = lambda i, rows=rows: rows[i // 4 : i // 4 + 1, i % 4 * share : (i % 4 + 1) * share]
        place = pl.ds(pl.multiple_of(device * share, share), share)
        for i in range(8):
            lines_ref[i : i + 1, place] = piece(i if i < 3 else i + extra)
        for e in range(extra):
            start = pl.multiple_of((device * extra + e) * share, share)
            up_ref[:, pl.ds(start, share)] = piece(3 + e)
    lines_ref[EMBED : EMBED + 1, :] = embeds_ref[pl.ds(at[CHIP], 1), :]
    lines_ref[WEIGHT:LINES, :] = jnp.broadcast_to(weight_ref[...], (LINES - WEIGHT, D))


def key_value_kernel(at, mine_ref, got_ref, lines_ref, *refs):
    *pieces, keys_ref, values_ref, weight_ref, rounded_ref = refs
    j = pl.program_id(0)

    @pl.when(j == 0)
    def _():
        half = mine_ref.shape[0]
        embed = line(lines_ref, EMBED)
        rounded_ref[:half, :] = (mine_ref[...].astype(F32) + embed).astype(BF16)
        rounded_ref[half:, :] = (got_ref[...].astype(F32) + embed).astype(BF16)

    product = dot(rounded_ref[...], order_rows(at, pieces, weight_ref))

    @pl.when(j == 0)
    def _():
        keys_ref[...] = product.astype(BF16)

    @pl.when(j == 1)
    def _():
        values_ref[...] = (product + line(lines_ref, VALUE_BIAS)).astype(BF16)


def query_kernel(at, rounded_ref, lines_ref, *refs):
    *pieces, _, out_ref, weight_ref = refs
    weight = order_rows(at, pieces, weight_ref)
    out_ref[...] = (dot(rounded_ref[...], weight) + line(lines_ref, QUERY_BIAS)).astype(BF16)


def head_mask(head):
    return lax.broadcasted_iota(jnp.int32, (1, GROUP), 1) // HEAD_DIM == head


def attend_kernel(_, q_ref, k1_ref, v1_ref, k2_ref, v2_ref, *refs):
    out_ref, lse_ref = refs[-2:]
    keys = jnp.concatenate([k1_ref[...], k2_ref[...]], axis=0)
    values_t = jnp.concatenate([v1_ref[...], v2_ref[...]], axis=0).T
    queries = q_ref[...] * jnp.asarray(HEAD_DIM**-0.5, BF16)
    outs = []
    for head in range(GROUP_HEADS):
        masked = jnp.where(head_mask(head), queries, jnp.zeros_like(queries))
        scores = dot_back(keys, masked)
        peak = jnp.max(scores, axis=0, keepdims=True)
        exponent = jnp.exp(scores - peak)
        summed = total(exponent)
        attention = (exponent * (1.0 / summed)).astype(BF16)
        lse_ref[0, head : head + 1, :] = peak + jnp.log(summed)
        outs.append(dot(values_t[head * HEAD_DIM : (head + 1) * HEAD_DIM, :], attention))
    out_ref[...] = jnp.concatenate(outs, axis=0).astype(BF16).T


def output_kernel(at, rounded_ref, mixed_ref, mine_ref, got_ref, lines_ref, *refs):
    *pieces, weight_ref, unit_ref, scale_ref, low_ref, away_ref = refs
    product = dot(mixed_ref[...], order_rows(at, pieces, weight_ref))
    half = mine_ref.shape[0]
    for start, tokens_ref in ((0, mine_ref), (half, got_ref)):
        place = pl.ds(start, half)
        hidden = tokens_ref[...].astype(F32) + line(lines_ref, EMBED)
        unit, scale = normalise(hidden + (product[start : start + half, :] + line(lines_ref, OUTPUT_BIAS)))
        unit_ref[place, :] = unit
        scale_ref[place, :] = scale
        low_ref[place, :] = (unit * line(lines_ref, GAIN1) + line(lines_ref, SHIFT1)).astype(BF16)
    width = D // 4
    for k, left_ref in enumerate((low_ref, rounded_ref, mixed_ref)):
        for flip in (1, 0):
            column = pl.multiple_of(their(flip, at) * width, width)
            block = 2 * k + 1 - flip
            away_ref[:, block * width : (block + 1) * width] = left_ref[:, pl.ds(column, width)]


def feed_forward_kernel(
    at, low_ref, bias_ref, unit1_ref, scale1_ref, mine_ref, got_ref, lines_ref, down_ref, output_ref, *refs
):
    pieces, refs = refs[:4], refs[4:]
    active_ref, active_away_ref, final_ref, away_ref, delta_ref, up_delta_ref, down_sums_ref, up_sums_ref = refs[:8]
    input_ref, out_ref, rights_ref, mixed_ref, first_sums_ref, up_all, active_all, slope_all, sum_ref = refs[8:]
    j = pl.program_id(0)
    row = lambda i: line(lines_ref, i)
    half = mine_ref.shape[0]

    @pl.when(j < 4)
    def _():
        weight = order_rows(at, pieces, up_all.at[j])
        for start in (0, half):
            place = pl.ds(start, half)
            active, slope = gelu_and_slope(dot(low_ref[place, :], weight) + bias_ref[...])
            active_ref[place, :] = active.astype(BF16)
            slope_all[j, place, :] = slope.astype(BF16)
        active_all[j] = active_ref[...]

    for flip in (1, 0):

        @pl.when(j == their(flip, at))
        def _(flip=flip):
            width = active_ref.shape[1]
            active_away_ref[:, (1 - flip) * width : (2 - flip) * width] = active_ref[...]

    @pl.when(j == 4)
    def _():
        sum_ref[...] = dot(active_all[0], down_ref[...])

    @pl.when((j > 4) & (j < 8))
    def _():
        sum_ref[...] += dot(active_all[j - 4], down_ref[...])

    @pl.when(j == 7)
    def _():
        sums = [0.0, 0.0, 0.0]
        for start, upstream_ref, one_ref in ((0, mine_ref, final_ref), (half, got_ref, away_ref)):
            place = pl.ds(start, half)
            first_norm = unit1_ref[place, :] * row(GAIN1) + row(SHIFT1)
            unit, scale = normalise(first_norm + (sum_ref[place, :] + row(DOWN_BIAS)))
            one_ref[...] = (unit * row(GAIN2) + row(SHIFT2)).astype(BF16)
            cotangent = upstream_ref[...].astype(F32) * row(WEIGHT)
            grad = normalise_back(unit, scale, row(GAIN2), cotangent)
            delta = grad.astype(BF16)
            sum_ref[place, :] = grad
            delta_ref[place, :] = delta
            parts = (cotangent * unit, cotangent, delta.astype(F32))
            sums = [one + total(part) for one, part in zip(sums, parts)]
        for i, one in enumerate(sums):
            down_sums_ref[i : i + 1, :] = one

    @pl.when(j >= 8)
    def _():
        k = j - 8
        delta = (dot_back(delta_ref[...], down_ref[...]) * slope_all[k].astype(F32)).astype(BF16)
        up_delta_ref[...] = delta
        up_sums_ref[pl.ds(k, 1), :] = total(delta.astype(F32))
        sum_ref[...] += dot_back(delta, up_all[k])

    @pl.when(j == 11)
    def _():
        sums = [0.0, 0.0, 0.0]
        for start in (0, half):
            place = pl.ds(start, half)
            grad, unit = sum_ref[place, :], unit1_ref[place, :]
            below = normalise_back(unit, scale1_ref[place, :], row(GAIN1), grad)
            delta = below.astype(BF16)
            input_ref[place, :] = below
            out_ref[place, :] = delta
            rights_ref[place, :] = delta
            mixed_ref[place, :] = dot_back(delta, output_ref[...]).astype(BF16)
            parts = (grad * unit, grad, delta.astype(F32))
            sums = [one + total(part) for one, part in zip(sums, parts)]
        for i, one in enumerate(sums):
            first_sums_ref[i : i + 1, :] = one


def attend_back_kernel(
    _, q_ref, k1_ref, v1_ref, k2_ref, v2_ref, lse_ref, grad_ref, *refs
):
    dq_ref, rights_ref, near_ref, far_ref, p_all, ds_all = refs[-6:]
    half, tokens = k1_ref.shape[0], q_ref.shape[0]
    keys = jnp.concatenate([k1_ref[...], k2_ref[...]], axis=0)
    values = jnp.concatenate([v1_ref[...], v2_ref[...]], axis=0)
    keys_t = keys.T
    queries = q_ref[...] * jnp.asarray(HEAD_DIM**-0.5, BF16)
    grads = grad_ref[...]
    query_parts, grad_parts, dq_parts = [], [], []
    for head in range(GROUP_HEADS):
        query_one = jnp.where(head_mask(head), queries, jnp.zeros_like(queries))
        grad_one = jnp.where(head_mask(head), grads, jnp.zeros_like(grads))
        attention = jnp.exp(dot_back(keys, query_one) - lse_ref[0, head : head + 1, :])
        prob_grad = dot_back(values, grad_one)
        weighted = total(attention * prob_grad)
        score_grad = (attention * (prob_grad - weighted)).astype(BF16)
        place = slice(head * tokens, (head + 1) * tokens)
        p_all[:, place] = attention.astype(BF16)
        ds_all[:, place] = score_grad
        dq_parts.append(dot(keys_t[head * HEAD_DIM : (head + 1) * HEAD_DIM, :], score_grad))
        query_parts.append(query_one)
        grad_parts.append(grad_one)
    value_grad = dot(p_all[...], jnp.concatenate(grad_parts, axis=0))
    key_grad = dot(ds_all[...], jnp.concatenate(query_parts, axis=0))
    dq_ref[...] = (jnp.concatenate(dq_parts, axis=0) * HEAD_DIM**-0.5).astype(BF16).T
    rights_ref[...] = dq_ref[...]
    near_ref[:, :GROUP] = key_grad[:half, :]
    near_ref[:, GROUP:] = value_grad[:half, :]
    far_ref[:, :GROUP] = key_grad[half:, :].astype(BF16)
    far_ref[:, GROUP:] = value_grad[half:, :].astype(BF16)


def delta_kernel(_, *refs):
    groups = D // GROUP
    nears, fars = refs[:groups], refs[groups : 2 * groups]
    queries_ref, __, keys_ref, values_ref, rights_ref, sums_ref = refs[2 * groups :]
    i = pl.program_id(0)
    for g in range(groups):
        place = slice(g * GROUP, (g + 1) * GROUP)
        rights_ref[:, place] = (nears[g][...] + fars[g][...].astype(F32)).astype(BF16)
    sums_ref[pl.ds(1 + i, 1), :] = total(rights_ref[...].astype(F32))

    @pl.when(i == 0)
    def _():
        sums_ref[0:1, :] = total(queries_ref[...].astype(F32))
        keys_ref[...] = rights_ref[...]

    @pl.when(i == 1)
    def _():
        values_ref[...] = rights_ref[...]


def input_query_kernel(_, delta_ref, weight_ref, grad_ref, out_ref):
    out_ref[...] = grad_ref[...] + dot_back(delta_ref[...], weight_ref[...])


def input_kernel(_, delta_ref, weight_ref, grad_ref, mine_ref, away_ref, time_ref, sum_ref):
    j = pl.program_id(0)
    part = dot_back(delta_ref[...], weight_ref[...])

    @pl.when(j == 0)
    def _():
        sum_ref[...] = grad_ref[...] + part

    @pl.when(j > 0)
    def _():
        sum_ref[...] += part

    @pl.when(j == pl.num_programs(0) - 1)
    def _():
        half = mine_ref.shape[0]
        mine_ref[...] = sum_ref[:half, :]
        away_ref[...] = sum_ref[half:, :].astype(BF16)
        time_ref[...] = total(sum_ref[...])


def grad_block(which, left_ref, right_ref, far_left_ref, fars, sum_ref, *more):
    for k, far_ref in enumerate(fars):

        @pl.when((which == k) if len(fars) > 1 else (which >= 0))
        def _(far_ref=far_ref):
            sum_ref[...] = outer(far_left_ref[...], far_ref[...])

    block = outer(left_ref[...], right_ref[...]) + sum_ref[...]
    for one_ref in more:
        block = block + one_ref[...].astype(F32)
    return block.astype(BF16)


def grad_x_kernel(_, left_ref, right_ref, far_left_ref, *refs):
    *fars, out_ref, sum_ref = refs
    out_ref[...] = grad_block(pl.program_id(0), left_ref, right_ref, far_left_ref, fars, sum_ref)


def grad_y_kernel(at_ref, left_ref, right_ref, far_left_ref, other_ref, *refs):
    *fars, away_ref, keep_ref, sum_ref = refs
    i, half = pl.program_id(0), pl.num_programs(0) // 2
    which = jnp.where(i < half, 1 - at_ref[SIDE_Y], at_ref[SIDE_Y])
    block = grad_block(which, left_ref, right_ref, far_left_ref, fars, sum_ref, other_ref)

    @pl.when(i < half)
    def _():
        away_ref[...] = block

    @pl.when(i >= half)
    def _():
        keep_ref[...] = block


def fold_kernel(_, keep1_ref, keep2_ref, away1_ref, away2_ref, keep_ref, away_ref):
    keep_ref[...] = (keep1_ref[...].astype(F32) + keep2_ref[...].astype(F32)).astype(BF16)
    away_ref[...] = (away1_ref[...].astype(F32) + away2_ref[...].astype(F32)).astype(BF16)


def add_kernel(_, one_ref, two_ref, out_ref):
    out_ref[...] = (one_ref[...].astype(F32) + two_ref[...].astype(F32)).astype(out_ref.dtype)


def join_kernel(at_ref, mine_ref, other_ref, out_ref):
    rows = mine_ref.shape[0]
    out_ref[pl.ds(pl.multiple_of(at_ref[SIDE_Z] * rows, 16), rows), :] = mine_ref[...]
    out_ref[pl.ds(pl.multiple_of((1 - at_ref[SIDE_Z]) * rows, 16), rows), :] = other_ref[...]


def finish_kernel(_, mine_ref, other_ref, *refs):
    out_ref = refs[-1]
    i, half = pl.program_id(0), pl.num_programs(0) // 2

    @pl.when(i < half)
    def _():
        out_ref[...] = mine_ref[...].astype(F32)

    @pl.when(i >= half)
    def _():
        out_ref[...] = other_ref[...].astype(F32)


def copy_kernel(_, in_ref, out_ref):
    out_ref[...] = in_ref[...]


def two_kernel(at, mine_ref, other_ref, first_ref, second_ref):
    first = at[SIDE_Y] == 0
    mine, other = mine_ref[...].astype(F32), other_ref[...].astype(F32)
    first_ref[...] = jnp.where(first, mine, other)
    second_ref[...] = jnp.where(first, other, mine)


def pair_kernel(_, mine_ref, received_ref, out_ref):
    @pl.when(pl.program_id(0) == 0)
    def _():
        out_ref[...] = mine_ref[...]

    @pl.when(pl.program_id(0) == 1)
    def _():
        out_ref[...] = received_ref[...].astype(out_ref.dtype)


def append_kernel(_, first_ref, *refs):
    *vectors, out_ref, small_ref = refs
    rows = first_ref.shape[0]
    out_ref[:rows, :] = first_ref[...]
    flat = jnp.concatenate([vector[...].astype(F32).reshape(1, -1) for vector in vectors], axis=1)
    lines = [flat[:, start : start + D] for start in range(0, flat.shape[1], D)]
    small = jnp.concatenate(lines + [jnp.zeros((16 - len(lines), D), F32)], axis=0).astype(BF16)
    small_ref[...] = small
    out_ref[rows:, :] = small


def side_by_side_kernel(_, *refs):
    out_ref, at = refs[-1], 0
    for piece in refs[:-1]:
        out_ref[:, at : at + piece.shape[1]] = piece[...]
        at += piece.shape[1]


def split_kernel(_, in_ref, first_ref, second_ref):
    rows = first_ref.shape[0]
    first_ref[...] = in_ref[:rows, :]
    second_ref[...] = in_ref[rows:, :]


def parity(at):
    return (at[SIDE_Y] + at[SIDE_Z]) % 2


def remote_kernel(at, half_ref, third_ref, fourth_ref, *outs):
    columns = 0
    for out_ref in outs:
        width = out_ref.shape[1]
        place = slice(columns, columns + width)
        columns += width
        remote_rows(at, half_ref.at[:, place], third_ref.at[:, place], fourth_ref.at[:, place], out_ref)


def remote_rows(at, half_ref, third_ref, fourth_ref, out_ref):
    half, quarter = half_ref.shape[0], third_ref.shape[0]
    missing = (1 - parity(at)) * half
    out_ref[pl.ds(pl.multiple_of(parity(at) * half, 16), half), :] = half_ref[...]
    out_ref[pl.ds(pl.multiple_of(missing, 16), quarter), :] = third_ref[...]
    out_ref[pl.ds(pl.multiple_of(missing + quarter, 16), quarter), :] = fourth_ref[...]


def lines_kernel(at, down_ref, first_ref, delta_ref, up_ref, time_ref, out_ref):
    out_ref[0:8, :] = down_ref[...]
    out_ref[8:16, :] = first_ref[...]
    out_ref[16:24, :] = delta_ref[...]
    out_ref[24:28, :] = up_ref[0:4, :]
    row = lax.broadcasted_iota(jnp.int32, (4, D), 0)
    out_ref[28:32, :] = jnp.where(row == at[CHIP], time_ref[...], 0.0)


def per_device(n_dp, inputs, timestep, bucket_count, upstream, *params):
    query_weight, key_weight, value_weight, output_weight, up_weight, down_weight = params[:6]
    vectors = params[6:]
    device = lax.axis_index("fsdp")
    chip, core = device // 2, device % 2
    bucket = lax.axis_index("dp")
    half = inputs.shape[1]
    tokens = 2 * half
    hidden_width = up_weight.shape[1]
    side_y, side_z = bucket % 2, (bucket // 2) % 2
    place = jnp.stack([chip, core, side_y, side_z]).astype(jnp.int32)
    run = functools.partial(run_kernel, place)

    def swap(value, axis, bit):
        size = 4 if axis == "fsdp" else n_dp
        return lax.ppermute(value, axis, [(i, i ^ bit) for i in range(size)])

    swap_core = lambda value: swap(value, "fsdp", 1)
    swap_chip = lambda value: swap(value, "fsdp", 2)
    swap_y = lambda value: swap(value, "dp", 1)
    swap_z = lambda value: swap(value, "dp", 2)

    def pick(array, flip, *later_than):
        _, rows, columns = array.shape
        ins = [(array, (None, rows, columns), lambda _, at: (at[CHIP] ^ flip, 0, 0))]
        return run("pick", copy_kernel, (1,), ins, [whole_out((rows, columns), array.dtype)], later_than)

    def pack(arrays, *later_than):
        shape = (arrays[0].shape[0], sum(array.shape[1] for array in arrays))
        return run("pack", side_by_side_kernel, (1,), [whole(a) for a in arrays], [whole_out(shape, BF16)], later_than)

    def cut(shards, *later_than):
        rows = shards[0].shape[0]
        columns = sum(shard.shape[1] for shard in shards)
        ins = [(shard, (rows // 2, shard.shape[1]), lambda _, at: (parity(at), 0)) for shard in shards]
        outs = [whole_out((rows // 2, columns), BF16)]
        return run("cut", side_by_side_kernel, (1,), ins, outs, later_than)

    def split(first, *later_than):
        rows, columns = first.shape
        outs = [whole_out((rows // 2, columns), BF16)] * 2
        to_y, to_z = run("split", split_kernel, (1,), [whole(first)], outs, later_than)
        return (first, swap_y(to_y), swap_z(to_z)), to_y

    def remote(parts, widths, *later_than):
        outs = [whole_out((2 * parts[0].shape[0], width), BF16) for width in widths]
        return run("remote", remote_kernel, (1,), [whole(part) for part in parts], outs, later_than)

    tokens_away, small = run(
        "pick", append_kernel, (1,),
        [(inputs, (None, half, D), lambda _, at: (at[CHIP] ^ 1, 0, 0))] + [whole(vector) for vector in vectors],
        [whole_out((half + 16, D), BF16), whole_out((16, D), BF16)],
    )
    tokens_got = swap_chip(tokens_away)
    got_half = (tokens_got, (half, D), lambda *_: (0, 0))
    three = (query_weight, key_weight, value_weight)
    two_weights = (output_weight, up_weight)
    three_cut = cut(three, tokens_away)
    three_first = swap_chip(three_cut)
    three_own = pack(three, three_cut)
    three_sibling = swap_core(three_own)
    two_own = pack(two_weights, three_own)
    two_sibling = swap_core(two_own)
    two_cut = cut(two_weights, tokens_got, two_own)
    two_first = swap_chip(two_cut)
    down_copy = run("copy", copy_kernel, (1,), [whole(down_weight)], [whole_out(down_weight.shape, BF16)], (two_cut,))
    live = chip < bucket_count[bucket]
    seq_weight = live.astype(F32) * (2 * n_dp / jnp.sum(bucket_count).astype(F32))
    small_two = jnp.concatenate([small, tokens_got[half:]], axis=0)
    small_far = swap_core(small_two)
    three_parts, split_done = split(three_first, three_sibling, two_sibling, down_copy, small_far)
    down_matrix = lax.all_gather(down_copy, "fsdp", axis=0, tiled=True)
    tokens_mine = pick(inputs, 0, split_done)
    query_remote, kv_remote = remote(three_parts, (D, 2 * D), tokens_mine)
    lines, up_bias = run(
        "lines_in", lines_in_kernel, (1,),
        [whole(a) for a in (small_two, small_far, sinusoid(timestep), seq_weight.reshape(1, 1))],
        [whole_out((LINES, D), F32), whole_out((1, hidden_width), F32)], (kv_remote,),
    )
    kv_pieces = [three_own, kv_remote, three_sibling, swap_core(kv_remote)]
    query_pieces = [three_own, query_remote, three_sibling, swap_core(query_remote)]
    keys, values, qkv_matrix, lefts = run(
        "key_value", key_value_kernel, (2,),
        [whole(tokens_mine), got_half, whole(lines)] + pieces_in(kv_pieces, D, (1, 0, 1, 0)),
        [
            whole_out((tokens, D), BF16),
            whole_out((tokens, D), BF16),
            ((D, 3 * D), BF16, (D, D), lambda j, *_: (0, 1 + j)),
            ((tokens, 2 * D), BF16, (tokens, D), lambda j, *_: (0, 0)),
        ],
    )
    far_keys, far_values = swap_core(keys), swap_core(values)
    queries, qkv_matrix = run(
        "query", query_kernel, (1,),
        [(lefts, (tokens, D), lambda j, *_: (0, 0)), whole(lines)] + pieces_in(query_pieces, D, (0, 0, 0, 0))
        + [(qkv_matrix, None, None)],
        [((tokens, D), BF16, (tokens, D), lambda j, *_: (0, 0)), ((D, 3 * D), BF16, (D, D), lambda j, *_: (0, 0))],
        aliases={2 + len(query_pieces): 1},
    )
    groups = D // GROUP
    group_of = lambda array, first: (array, (array.shape[0], GROUP), lambda g, *_: (0, first + g))

    def attend(first, count, lefts, lse, *later_than):
        return run(
            "attend", attend_kernel, (count,),
            [group_of(a, first) for a in (queries, keys, values, far_keys, far_values)] + [(lefts, None, None)]
            + ([] if lse is None else [(lse, None, None)]),
            [
                ((tokens, 2 * D), BF16, (tokens, GROUP), lambda g, *_: (0, groups + first + g)),
                ((groups, GROUP_HEADS, tokens), F32, (1, GROUP_HEADS, tokens), lambda g, *_: (first + g, 0, 0)),
            ],
            later_than, aliases={5: 0} if lse is None else {5: 0, 6: 1}, vmem=32,
        )

    lefts, lse = attend(0, groups // 2, lefts, None)
    two_parts, split_done = split(two_first, lse)
    upstream_away = pick(upstream, 1, split_done)
    upstream_got = swap_chip(upstream_away)
    lefts, lse = attend(groups // 2, groups // 2, lefts, lse, upstream_away)
    two_remote = remote(two_parts, (two_own.shape[1],), lse)
    upstream_mine = pick(upstream, 0, two_remote)
    two_pieces = [two_own, two_remote, two_sibling, swap_core(two_remote)]
    output_matrix, unit1, scale1, first_low, lefts_away = run(
        "output", output_kernel, (1,),
        [(lefts, (tokens, D), lambda j, *_: (0, 0)), (lefts, (tokens, D), lambda j, *_: (0, 1))]
        + [whole(tokens_mine), got_half, whole(lines)]
        + pieces_in(two_pieces, D, (0, 0, 0, 0)),
        [
            whole_out((D, D), BF16),
            whole_out((tokens, D), F32),
            whole_out((tokens, 1), F32),
            whole_out((tokens, D), BF16),
            whole_out((tokens, 6 * D // 4), BF16),
        ],
        (upstream_mine,),
    )
    lefts_away = swap_core(lefts_away)
    width = hidden_width // 4
    hidden_block = lambda j: jnp.minimum(j, 3)
    results = run(
        "feed_forward", feed_forward_kernel, (12,),
        [held(first_low), (up_bias, (1, width), lambda j, *_: (0, hidden_block(j))), held(unit1), held(scale1)]
        + [held(upstream_mine), held(upstream_got), held(lines)]
        + [(down_matrix, (width, D), lambda j, *_: (jnp.where(j < 4, 0, j % 4), 0)), held(output_matrix)]
        + [(piece, (piece.shape[0], width), lambda j, *_: (0, D // width + hidden_block(j))) for piece in two_pieces],
        [
            ((tokens, hidden_width), BF16, (tokens, width), lambda j, *_: (0, hidden_block(j))),
            whole_out((tokens, 2 * width), BF16),
            whole_out((half, D), BF16),
            whole_out((half, D), BF16),
            whole_out((tokens, D), BF16),
            ((tokens, hidden_width), BF16, (tokens, width), lambda j, *_: (0, jnp.maximum(j - 8, 0))),
            whole_out((8, D), F32),
            whole_out((8, D), F32),
            whole_out((tokens, D), F32),
            whole_out((tokens, D), BF16),
            ((tokens, 4 * D), BF16, (tokens, D), lambda j, *_: (0, 3)),
            whole_out((tokens, D), BF16),
            whole_out((8, D), F32),
        ],
        (),
        [
            pltpu.VMEM((4, D, width), BF16),
            pltpu.VMEM((4, tokens, width), BF16),
            pltpu.VMEM((4, tokens, width), BF16),
            pltpu.VMEM((tokens, D), F32),
        ],
    )
    activated, active_away, final_mine, final_away, down_delta, up_delta, down_sums, up_sums = results[:8]
    input_part, out_delta, rights, mixed_grad, first_sums = results[8:]
    active_away, down_far = swap_core(active_away), swap_core(down_delta)
    up_far, out_far = swap_core(up_delta), swap_core(out_delta)

    block_rows = D // 4

    class Grads:
        def __init__(self, left, right, send, keep, fars, near, right_column):
            self.left, self.right, self.send_far, self.keep_far = left, right, send, keep
            self.fars, self.near, self.right_column = fars, near, right_column

        def ins(self, flip, far, block):
            far_left, far_column = far
            shard = lambda at: 2 * (at[CHIP] ^ flip) + at[CORE]
            return [
                (self.left, (tokens, block_rows), lambda i, at: (0, self.near(shard(at), block(i, at)))),
                (self.right, (tokens, D), lambda i, at: (0, self.right_column(block(i, at)))),
                (far_left, (tokens, block_rows), lambda i, at: (0, far_column(block(i, at)))),
            ]

        def far_ins(self, block, first, count):
            if len(self.fars) > 1:
                return [whole(a) for a in self.fars[first : first + count]]
            return [(self.fars[0], (tokens, D), lambda i, at: (0, self.right_column(block(i, at))))]

        def four(self, name, body, flip, far, more, *later_than):
            out = ((4 * block_rows, D), BF16, (block_rows, D), lambda i, at: (i, 0))
            block = lambda i, at: i
            ins = self.ins(flip, far, block) + more + self.far_ins(block, 0, 4)
            return run(name, body, (4,), ins, [out], later_than, [pltpu.VMEM((block_rows, D), F32)])

        def start(self, *later_than):
            sent = self.four("grad_x", grad_x_kernel, 1, self.send_far, [], *later_than)
            self.got = swap_chip(sent)
            return sent

    class Chunk:
        def __init__(self, grads, first, count):
            self.grads, self.first, self.half = grads, first, count // 2

        def over_y(self, last):
            grads, first, half = self.grads, self.first, self.half
            block = lambda i, at: first + jnp.where(
                i < half, (1 - at[SIDE_Y]) * half + i, at[SIDE_Y] * half + i - half
            )
            other = (grads.got, (block_rows, D), lambda i, at: (block(i, at), 0))
            shape = (half * block_rows, D)
            away, self.keep = run(
                "grad_y", grad_y_kernel, (2 * half,),
                grads.ins(0, grads.keep_far, block) + [other] + grads.far_ins(block, first, 2),
                [
                    (shape, BF16, (block_rows, D), lambda i, at: (jnp.minimum(i, half - 1), 0)),
                    (shape, BF16, (block_rows, D), lambda i, at: (jnp.maximum(i - half, 0), 0)),
                ],
                (last,), [pltpu.VMEM((block_rows, D), F32)],
            )
            self.got = swap_y(away)
            return self.keep

        def over_z(self, last):
            block = (self.keep.shape[0] // 2, D)
            kept = [(a, block, lambda _, at: (at[SIDE_Z], 0)) for a in (self.keep, self.got)]
            given = [(a, block, lambda _, at: (1 - at[SIDE_Z], 0)) for a in (self.keep, self.got)]
            self.keep, away = run("grad_z", fold_kernel, (1,), kept + given, [whole_out(block, BF16)] * 2, (last,))
            self.got = swap_z(away)
            return self.keep

        def add(self, bit, last):
            ins = [whole(self.keep), whole(self.got)]
            self.keep = run("grad_add", add_kernel, (1,), ins, [whole_out(self.keep.shape, BF16)], (last,))
            self.got = swap(self.keep, "dp", bit)
            return self.keep

        def add_high(self, last):
            for bit in high_bits:
                last = self.add(bit, last)
            return last

        def add_low(self, last):
            return self.add(2, last)

        def back(self, last):
            ins = [whole(self.keep), whole(self.got)]
            shape = (2 * self.keep.shape[0], D)
            self.keep = run("grad_join", join_kernel, (1,), ins, [whole_out(shape, BF16)], (last,))
            self.got = swap_y(self.keep)
            return self.keep

        def finish(self, last, shape, index):
            half = self.half
            ins = [
                (self.keep, (block_rows, D), lambda i, at: (jnp.minimum(i, half - 1), 0)),
                (self.got, (block_rows, D), lambda i, at: (jnp.maximum(i - half, 0), 0)),
            ]
            place = lambda i, at: jnp.where(i < half, at[SIDE_Y] * half + i, (1 - at[SIDE_Y]) * half + i - half)
            out = (shape, F32, (block_rows, D), lambda i, at: index(place(i, at)))
            return run("grad_out", finish_kernel, (2 * half,), ins, [out], (last,))

    def pair_of(mine, received, dtype, last):
        out = ((2, half, D), dtype, (None, half, D), lambda i, at: (at[CHIP] ^ i, 0, 0))
        return run("pair", pair_kernel, (2,), [whole(mine), whole(received)], [out], (last,))

    high_bits = [1 << i for i in range(2, n_dp.bit_length()) if 1 << i < n_dp]
    relay = lambda array, last: run("relay", copy_kernel, (1,), [whole(array)], [whole_out(array.shape, array.dtype)], (last,))

    grads_down = Grads(
        activated, down_delta, (active_away, lambda b: b), (active_away, lambda b: 4 + b), [down_far],
        lambda shard, b: shard * (hidden_width // D) + b, lambda b: 0,
    )
    grads_up = Grads(
        first_low, up_delta, (lefts_away, lambda b: 0), (lefts_away, lambda b: 1), [up_far],
        lambda shard, b: shard, lambda b: b,
    )

    def attend_back(first, count, later_than, rights, query_delta):
        return run(
            "attend_back", attend_back_kernel, (count,),
            [group_of(a, first) for a in (queries, keys, values, far_keys, far_values)]
            + [(lse, (1, GROUP_HEADS, tokens), lambda g, *_: (first + g, 0, 0)), group_of(mixed_grad, first)]
            + [(rights, None, None)] + ([] if query_delta is None else [(query_delta, None, None)]),
            [
                ((tokens, D), BF16, (tokens, GROUP), lambda g, *_: (0, first + g)),
                ((tokens, 4 * D), BF16, (tokens, GROUP), lambda g, *_: (0, first + g)),
                ((tokens, 2 * count * GROUP), F32, (tokens, 2 * GROUP), lambda g, *_: (0, g)),
                ((tokens, 2 * count * GROUP), BF16, (tokens, 2 * GROUP), lambda g, *_: (0, g)),
            ],
            later_than, [pltpu.VMEM((2 * tokens, GROUP_HEADS * tokens), BF16)] * 2, aliases={7: 1} if query_delta is None else {7: 1, 8: 0},
        )

    first_call = 1
    query_delta, rights, near1, far1 = attend_back(0, first_call, (mixed_grad,), rights, None)
    far1 = swap_core(far1)
    last = grads_down.start(near1)
    last = grads_up.start(last, out_far)
    query_delta, rights, near2, far2 = attend_back(first_call, groups - first_call, (last, far1), rights, query_delta)
    far2, query_far = swap_core(far2), swap_core(query_delta)
    last = input_part = run(
        "input_query", input_query_kernel, (2,),
        [
            (query_delta, (half, D), lambda i, *_: (i, 0)),
            (qkv_matrix, (D, D), lambda i, *_: (0, 0)),
            (input_part, (half, D), lambda i, *_: (i, 0)),
        ],
        [((tokens, D), F32, (half, D), lambda i, *_: (i, 0))], (near2,),
    )
    key_delta, value_delta, rights, delta_sums = run(
        "delta", delta_kernel, (2,),
        [
            (a, (tokens, GROUP), lambda i, *_, g=g: (0, 2 * g + i))
            for one, two in ((near1, near2), (far1, far2))
            for a, count in ((one, first_call), (two, groups - first_call))
            for g in range(count)
        ]
        + [whole(query_delta), (rights, None, None)],
        [
            whole_out((tokens, D), BF16),
            whole_out((tokens, D), BF16),
            ((tokens, 4 * D), BF16, (tokens, D), lambda i, *_: (0, 1 + i)),
            whole_out((8, D), F32),
        ],
        (last,), aliases={2 * groups + 1: 2},
    )
    key_far, value_far = swap_core(key_delta), swap_core(value_delta)
    step = D
    input_mine, input_away, time_sum = run(
        "input", input_kernel, (2,),
        [(rights, (tokens, D), lambda j, *_: (0, 1 + j)), (qkv_matrix, (D, D), lambda j, *_: (0, 1 + j)), whole(input_part)],
        [whole_out((half, D), F32), whole_out((half, D), BF16), whole_out((1, D), F32)],
        (delta_sums,), [pltpu.VMEM((tokens, D), F32)],
    )
    last_one = lambda b: jnp.where(b == 3, 1, 0)
    grads_four = Grads(
        lefts, rights, (lefts_away, lambda b: 2 + 2 * last_one(b)), (lefts_away, lambda b: 3 + 2 * last_one(b)),
        [query_far, key_far, value_far, out_far], lambda shard, b: shard + 4 * last_one(b), lambda b: b,
    )
    last = grads_four.start(time_sum)

    packed = run(
        "lines", lines_kernel, (1,), [whole(a) for a in (down_sums, first_sums, delta_sums, up_sums, time_sum)],
        [whole_out((32, D), F32)], (last,),
    )
    hops = [("fsdp", 1), ("fsdp", 2)] + [("dp", 1 << i) for i in range(n_dp.bit_length() - 1)]
    line_parts, line_got = [packed], [swap(packed, *hops[0])]

    def add_lines(last):
        ins = [whole(line_parts[-1]), whole(line_got[-1])]
        line_parts.append(run("lines_add", add_kernel, (1,), ins, [whole_out((32, D), F32)], (last,)))
        if len(line_parts) <= len(hops) - 0 and len(line_got) < len(hops):
            line_got.append(swap(line_parts[-1], *hops[len(line_got)]))
        return line_parts[-1]

    down, up = Chunk(grads_down, 0, 4), Chunk(grads_up, 0, 4)
    qk, vo = Chunk(grads_four, 0, 2), Chunk(grads_four, 2, 2)
    last = down.over_y(packed)
    last = add_lines(last)
    last = down.over_z(last)
    last = up.over_y(last)
    last = down.add_high(last)
    last = up.over_z(last)
    last = qk.over_y(last)
    last = vo.over_y(last)
    last = down.add_low(last)
    last = up.add_high(last)
    last = qk.over_z(last)
    last = vo.over_z(last)
    last = add_lines(last)
    last = final_away = relay(final_away, last)
    final_got = swap_chip(final_away)
    last = qk.add_high(last)
    last = vo.add_high(last)
    last = down.back(last)
    last = up.add_low(last)
    last = add_lines(last)
    last = qk.add_low(last)
    last = vo.add_low(last)
    last = final = pair_of(final_mine, final_got, BF16, last)
    last = input_away = relay(input_away, last)
    input_got = swap_chip(input_away)
    last = up.back(last)
    last = qk.back(last)
    last = vo.back(last)
    while len(line_parts) < len(hops):
        last = add_lines(last)
    last = down_grad = down.finish(last, down_weight.shape, lambda s: (s, 0))
    last = input_gradient = pair_of(input_mine, input_got, F32, last)
    last = up_grad = up.finish(last, up_weight.shape, lambda s: (0, s))
    last = add_lines(last)

    def two(chunk, last):
        outs = [whole_out((block_rows, D), F32)] * 2
        return run("two", two_kernel, (1,), [whole(chunk.keep), whole(chunk.got)], outs, (last,))

    query_grad, key_grad = two(qk, last)
    value_grad, output_grad = two(vo, query_grad)
    times = lax.dynamic_slice_in_dim(line_parts[2], device * (D // 4), D // 4, axis=1)
    time_gradient = times[28:30]
    packed = line_parts[-1]
    mine = lax.dynamic_slice_in_dim(packed, device * (D // 4), D // 4, axis=1)
    up_bias_grad = lax.dynamic_slice_in_dim(packed[24:28], device, 1, axis=0).reshape(-1)
    vector_grads = (mine[16], mine[18], mine[10], up_bias_grad, mine[2], mine[8], mine[9], mine[0], mine[1])

    return (
        final,
        input_gradient,
        time_gradient,
        query_grad,
        key_grad,
        value_grad,
        output_grad,
        up_grad,
        down_grad,
        *vector_grads,
    )


def solution(mesh):
    rows, wide, flat = P("dp", "fsdp", None), P("fsdp", None), P("fsdp")
    return jax.shard_map(
        functools.partial(per_device, mesh.shape["dp"]),
        mesh=mesh,
        in_specs=(rows, P("dp"), P(), rows) + (wide,) * 6 + (flat,) * 9,
        out_specs=(rows, rows, P("dp", "fsdp")) + (wide,) * 6 + (flat,) * 9,
        check_vma=False,
    )
```

profile of v0, /device:TPU:0, one launch (start us, length us, event | category | flops | bytes accessed | tf_op | source)
XLA Modules:
  0.0 479.2 jit_solution(14316548856670737217)
XLA Ops:
  37.9 6.2 %collective-permute-done.refs_1_ = bf16[128,3072]{1,0:T(8,128)(2,1)} collective-permute-done((bf16[128,3072]{1,0:T(8,128)(2,1)}, bf16[128,3072]{1,0:T(8,128)(2,1)}, u32[]{:S(2)}, u32[]{:S(2)}) %collective-permute-start) | collective-permute-done | bytes 786464 | tf_op jit(solution)/shard_map/ppermute | solution.py:547
  64.0 8.6 %key_value.1 = (bf16[512,1024]{1,0:T(8,128)(2,1)}, bf16[512,1024]{1,0:T(8,128)(2,1)}, bf16[1024,3072]{1,0:T(8,128)(2,1)}, bf16[512,2048]{1,0:T(8,128)(2,1)}) custom-call(s32[4]{0:T(128)} %pad_add_fusion.refs_0_, bf16[256,1024]{1,0:T(8,128)(2,1)} %pick.5.refs_4_.refs_1_.refs_3_, bf16[272,1024]{1,0:T(8,128)(2,1)} %collective-permute-done.3.refs_3_.refs_2_.refs_4_, ...), custom_call_target="tpu_custom_call" | custom-call | flops 699999977472 | tf_op jit(solution)/shard_map/key_value/pallas_call | solution.py:44
  78.1 10.8 %attend.2 = (bf16[512,2048]{1,0:T(8,128)(2,1)}, f32[4,4,512]{2,1,0:T(4,128)}) custom-call(s32[4]{0:T(128)} %pad_add_fusion.refs_0_, bf16[512,1024]{1,0:T(8,128)(2,1)} %get-tuple-element.100.refs_1_, bf16[512,1024]{1,0:T(8,128)(2,1)} %get-tuple-element.101.refs_2_, bf16[512,1024]{1,0:T(8,128)(2,1)} %get-tuple-element.102.refs_3_, ...), custom_call_target="tpu_custom_call", output_to_operand_aliasing={{0}: (6, {})} | custom-call | flops 899999989760 | tf_op jit(solution)/shard_map/attend/pallas_call | solution.py:44
  88.9 5.5 %collective-permute-done.11.refs_1_ = bf16[128,5120]{1,0:T(8,128)(2,1)} collective-permute-done((bf16[128,5120]{1,0:T(8,128)(2,1)}, bf16[128,5120]{1,0:T(8,128)(2,1)}, u32[]{:S(2)}, u32[]{:S(2)}) %collective-permute-start.11) | collective-permute-done | bytes 1310752 | tf_op jit(solution)/shard_map/ppermute | solution.py:547
  105.5 11.4 %attend.3 = (bf16[512,2048]{1,0:T(8,128)(2,1)}, f32[4,4,512]{2,1,0:T(4,128)}) custom-call(s32[4]{0:T(128)} %pad_add_fusion.refs_0_, bf16[512,1024]{1,0:T(8,128)(2,1)} %get-tuple-element.100.refs_1_, bf16[512,1024]{1,0:T(8,128)(2,1)} %get-tuple-element.101.refs_2_, ...), custom_call_target="tpu_custom_call", output_to_operand_aliasing={{0}: (6, {}), {1}: (7, {})} | custom-call | flops 899999989760 | tf_op jit(solution)/shard_map/attend/pallas_call | solution.py:44
  126.2 7.6 %output.1 = (bf16[1024,1024]{1,0:T(8,128)(2,1)}, f32[512,1024]{1,0:T(8,128)}, f32[512,1]{1,0:T(8,128)}, bf16[512,1024]{1,0:T(8,128)(2,1)}, bf16[512,1536]{1,0:T(8,128)(2,1)}) custom-call(s32[4]{0:T(128)} %pad_add_fusion.refs_0_, bf16[512,2048]{1,0:T(8,128)(2,1)} %get-tuple-element.106.refs_1_.refs_2_, bf16[512,2048]{1,0:T(8,128)(2,1)} %get-tuple-element.106.refs_1_.refs_2_, ...), custom_call_target="tpu_custom_call" | custom-call | flops 599999971328 | tf_op jit(solution)/shard_map/output/pallas_call | solution.py:44
  133.9 42.6 %feed_forward.1 = (bf16[512,4096]{1,0:T(8,128)(2,1)}, bf16[512,2048]{1,0:T(8,128)(2,1)}, bf16[256,1024]{1,0:T(8,128)(2,1)}, bf16[256,1024]{1,0:T(8,128)(2,1)}, b...) custom-call(s32[4]{0:T(128)} %pad_add_fusion.refs_0_, ...), custom_call_target="tpu_custom_call" | custom-call | flops 3999999983616 | tf_op jit(solution)/shard_map/feed_forward/pallas_call | solution.py:44
  177.6 10.1 %attend_back.2 = (bf16[512,1024]{1,0:T(8,128)(2,1)}, bf16[512,4096]{1,0:T(8,128)(2,1)}, f32[512,512]{1,0:T(8,128)}, bf16[512,512]{1,0:T(8,128)(2,1)}) custom-call(s32[4]{0:T(128)} %pad_add_fusion.refs_0_, bf16[512,1024]{1,0:T(8,128)(2,1)} %get-tuple-element.100.refs_1_, ...), custom_call_target="tpu_custom_call", output_to_operand_aliasing={{1}: (8, {})} | custom-call | flops 1500000026624 | tf_op jit(solution)/shard_map/attend_back/pallas_call | solution.py:44
  188.1 7.3 %grad_x.3.refs_5_ = bf16[1024,1024]{1,0:T(8,128)(2,1)} custom-call(s32[4]{0:T(128)} %pad_add_fusion.refs_0_, bf16[512,4096]{1,0:T(8,128)(2,1)} %get-tuple-element.125.refs_1_, bf16[512,1024]{1,0:T(8,128)(2,1)} %get-tuple-element.126.refs_2_, bf16[512,2048]{1,0:T(8,128)(2,1)} %collective-permute-done.18.refs_3_, ...), custom_call_target="tpu_custom_call" | custom-call | flops 799999983616 | tf_op jit(solution)/shard_map/grad_x/pallas_call | solution.py:44
  195.6 7.9 %grad_x.4.refs_10_ = bf16[1024,1024]{1,0:T(8,128)(2,1)} custom-call(s32[4]{0:T(128)} %pad_add_fusion.refs_0_, bf16[512,1024]{1,0:T(8,128)(2,1)} %get-tuple-element.109.refs_1_, bf16[512,4096]{1,0:T(8,128)(2,1)} %get-tuple-element.123.refs_2_, bf16[512,1536]{1,0:T(8,128)(2,1)} %collective-permute-done.16.refs_3_, ...), custom_call_target="tpu_custom_call" | custom-call | flops 799999983616 | tf_op jit(solution)/shard_map/grad_x/pallas_call | solution.py:44
  205.3 23.9 %attend_back.3 = (bf16[512,1024]{1,0:T(8,128)(2,1)}, bf16[512,4096]{1,0:T(8,128)(2,1)}, f32[512,1536]{1,0:T(8,128)}, bf16[512,1536]{1,0:T(8,128)(2,1)}) custom-call(s32[4]{0:T(128)} %pad_add_fusion.refs_0_, bf16[512,1024]{1,0:T(8,128)(2,1)} %get-tuple-element.100.refs_1_, ...), custom_call_target="tpu_custom_call", output_to_operand_aliasing={{1}: (8, {}), {0}: (9, {})} | custom-call | flops 1500000026624 | tf_op jit(solution)/shard_map/attend_back/pallas_call | solution.py:44
  229.7 5.2 %input_query.1.refs_11_.refs_3_ = f32[512,1024]{1,0:T(8,128)} custom-call(s32[4]{0:T(128)} %pad_add_fusion.refs_0_, bf16[512,1024]{1,0:T(8,128)(2,1)} %get-tuple-element.132.refs_1_.refs_9_, bf16[1024,3072]{1,0:T(8,128)(2,1)} %get-tuple-element.134.refs_2_, f32[512,1024]{1,0:T(8,128)} %get-tuple-element.135.refs_3_, ...), custom_call_target="tpu_custom_call" | custom-call | flops 499999997952 | tf_op jit(solution)/shard_map/input_query/pallas_call | solution.py:44
  235.0 6.7 %delta.1 = (bf16[512,1024]{1,0:T(8,128)(2,1)}, bf16[512,1024]{1,0:T(8,128)(2,1)}, bf16[512,4096]{1,0:T(8,128)(2,1)}, f32[8,1024]{1,0:T(8,128)}) custom-call(s32[4]{0:T(128)} %pad_add_fusion.refs_0_, f32[512,512]{1,0:T(8,128)} %get-tuple-element.120.refs_5_.refs_1_, ...), custom_call_target="tpu_custom_call", output_to_operand_aliasing={{2}: (10, {})} | custom-call | flops 499999997952 | tf_op jit(solution)/shard_map/delta/pallas_call | solution.py:44
  242.2 7.6 %input.1 = (f32[256,1024]{1,0:T(8,128)}, bf16[256,1024]{1,0:T(8,128)(2,1)}, f32[1,1024]{1,0:T(1,128)}) custom-call(s32[4]{0:T(128)} %pad_add_fusion.refs_0_, bf16[512,4096]{1,0:T(8,128)(2,1)} %get-tuple-element.138.refs_1_.refs_2_, bf16[1024,3072]{1,0:T(8,128)(2,1)} %get-tuple-element.134.refs_2_, f32[512,1024]{1,0:T(8,128)} %input_query.1.refs_11_.refs_3_, ...), custom_call_target="tpu_custom_call" | custom-call | flops 799999983616 | tf_op jit(solution)/shard_map/input/pallas_call | solution.py:44
  249.9 9.1 %grad_x.5.refs_6_ = bf16[1024,1024]{1,0:T(8,128)(2,1)} custom-call(s32[4]{0:T(128)} %pad_add_fusion.refs_0_, bf16[512,2048]{1,0:T(8,128)(2,1)} %get-tuple-element.106.refs_1_.refs_2_, bf16[512,4096]{1,0:T(8,128)(2,1)} %get-tuple-element.138.refs_1_.refs_2_, bf16[512,1536]{1,0:T(8,128)(2,1)} %collective-permute-done.16.refs_3_, ...), custom_call_target="tpu_custom_call" | custom-call | flops 799999983616 | tf_op jit(solution)/shard_map/grad_x/pallas_call | solution.py:44
  263.3 6.6 %grad_y.4 = (bf16[512,1024]{1,0:T(8,128)(2,1)S(1)}, bf16[512,1024]{1,0:T(8,128)(2,1)S(1)}) custom-call(s32[4]{0:T(128)S(1)} %copy-done, bf16[512,4096]{1,0:T(8,128)(2,1)S(1)} %copy-done.10, bf16[512,1024]{1,0:T(8,128)(2,1)S(1)} %copy-done.3, bf16[512,2048]{1,0:T(8,128)(2,1)} %collective-permute-done.18.refs_3_, ...), custom_call_target="tpu_custom_call" | custom-call | flops 499999997952 | tf_op jit(solution)/shard_map/grad_y/pallas_call | solution.py:44
  274.4 20.7 %collective-permute-done.31.refs_2_.refs_4_ = bf16[512,1024]{1,0:T(8,128)(2,1)S(1)} collective-permute-done((bf16[512,1024]{1,0:T(8,128)(2,1)S(1)}, bf16[512,1024]{1,0:T(8,128)(2,1)S(1)}, u32[]{:S(2)}, u32[]{:S(2)}) %collective-permute-start.31) | collective-permute-done | bytes 1048608 | tf_op jit(solution)/shard_map/ppermute | solution.py:547
  298.1 7.5 %grad_y.5 = (bf16[512,1024]{1,0:T(8,128)(2,1)}, bf16[512,1024]{1,0:T(8,128)(2,1)S(1)}) custom-call(s32[4]{0:T(128)S(1)} %copy-done, bf16[512,1024]{1,0:T(8,128)(2,1)S(1)} %copy-done.18, bf16[512,4096]{1,0:T(8,128)(2,1)S(1)} %copy-done.1, bf16[512,1536]{1,0:T(8,128)(2,1)} %collective-permute-done.16.refs_3_, ...), custom_call_target="tpu_custom_call" | custom-call | flops 499999997952 | tf_op jit(solution)/shard_map/grad_y/pallas_call | solution.py:44
  315.3 14.6 %collective-permute-done.32.refs_2_.refs_4_ = bf16[512,1024]{1,0:T(8,128)(2,1)} collective-permute-done((bf16[512,1024]{1,0:T(8,128)(2,1)}, bf16[512,1024]{1,0:T(8,128)(2,1)}, u32[]{:S(2)}, u32[]{:S(2)}) %collective-permute-start.32) | collective-permute-done | bytes 1048608 | tf_op jit(solution)/shard_map/ppermute | solution.py:547
  334.1 5.3 %grad_y.6 = (bf16[256,1024]{1,0:T(8,128)(2,1)}, bf16[256,1024]{1,0:T(8,128)(2,1)S(1)}) custom-call(s32[4]{0:T(128)S(1)} %copy-done, bf16[512,2048]{1,0:T(8,128)(2,1)S(1)} %copy-done.11, bf16[512,4096]{1,0:T(8,128)(2,1)S(1)} %copy-done.9, bf16[512,1536]{1,0:T(8,128)(2,1)} %collective-permute-done.16.refs_3_, ...), custom_call_target="tpu_custom_call" | custom-call | flops 499999997952 | tf_op jit(solution)/shard_map/grad_y/pallas_call | solution.py:44
  339.9 5.3 %grad_y.7 = (bf16[256,1024]{1,0:T(8,128)(2,1)}, bf16[256,1024]{1,0:T(8,128)(2,1)S(1)}) custom-call(s32[4]{0:T(128)S(1)} %copy-done, bf16[512,2048]{1,0:T(8,128)(2,1)S(1)} %copy-done.11, bf16[512,4096]{1,0:T(8,128)(2,1)S(1)} %copy-done.9, bf16[512,1536]{1,0:T(8,128)(2,1)} %collective-permute-done.16.refs_3_, ...), custom_call_target="tpu_custom_call" | custom-call | flops 499999997952 | tf_op jit(solution)/shard_map/grad_y/pallas_call | solution.py:44
  371.4 9.8 %collective-permute-done.40.refs_2_ = bf16[128,1024]{1,0:T(8,128)(2,1)} collective-permute-done((bf16[128,1024]{1,0:T(8,128)(2,1)}, bf16[128,1024]{1,0:T(8,128)(2,1)}, u32[]{:S(2)}, u32[]{:S(2)}) %collective-permute-start.40) | collective-permute-done | bytes 262176 | tf_op jit(solution)/shard_map/ppermute | solution.py:547
  437.6 5.0 %grad_out.2.refs_3_ = f32[1024,1024]{1,0:T(8,128)} custom-call(s32[4]{0:T(128)S(1)} %copy-done, bf16[512,1024]{1,0:T(8,128)(2,1)} %grad_join.4.refs_3_.refs_1_, bf16[512,1024]{1,0:T(8,128)(2,1)} %collective-permute-done.47.refs_2_, f32[32,1024]{1,0:T(8,128)} %lines_add.8.refs_3_.refs_1_), custom_call_target="tpu_custom_call" | custom-call | flops 299999985664 | tf_op jit(solution)/shard_map/grad_out/pallas_call | solution.py:44
  454.2 5.0 %grad_out.3.refs_3_ = f32[256,4096]{1,0:T(8,128)} custom-call(s32[4]{0:T(128)S(1)} %copy-done, bf16[512,1024]{1,0:T(8,128)(2,1)} %grad_join.5.refs_3_.refs_1_, bf16[512,1024]{1,0:T(8,128)(2,1)} %collective-permute-done.54.refs_2_, f32[2,256,1024]{2,1,0:T(8,128)S(1)} %copy-done.6), custom_call_target="tpu_custom_call" | custom-call | flops 299999985664 | tf_op jit(solution)/shard_map/grad_out/pallas_call | solution.py:44
  (220 shorter events, 212.8 us)
Async XLA Ops:
  7.2 126.7 %all-gather.2.cloned.1.call-start = ((), (), s32[]{:S(2)}) async-start(), calls=%async_computation | async-start | bytes 10485760 | tf_op jit(solution)/shard_map/all_gather | solution.py:603
  16.2 27.9 %collective-permute-start = (bf16[128,3072]{1,0:T(8,128)(2,1)}, bf16[128,3072]{1,0:T(8,128)(2,1)}, u32[]{:S(2)}, u32[]{:S(2)}) collective-permute-start(bf16[128,3072]{1,0:T(8,128)(2,1)} %cut.2.refs_4_), channel_id=1, source_target_pairs={{0,2},{1,3},{2,0},{3,1},{4,6},{5,7},{6,4},{7,5},{8,10},{9,11},{10,... | collective-permute-start | bytes 2359304 | tf_op jit(solution)/shard_map/ppermute | solution.py:547
  19.4 24.6 %collective-permute-start.1 = (bf16[256,3072]{1,0:T(8,128)(2,1)}, bf16[256,3072]{1,0:T(8,128)(2,1)}, u32[]{:S(2)}, u32[]{:S(2)}) collective-permute-start(bf16[256,3072]{1,0:T(8,128)(2,1)} %pack.2.refs_3_.refs_4_), channel_id=1, source_target_pairs={{0,1},{1,0},{2,3},{3,2},{4,5},{5,4},{6,7},{7,6},{8,9},{9,8},{10,11... | collective-permute-start | bytes 4718600 | tf_op jit(solution)/shard_map/ppermute | solution.py:547
  32.1 62.3 %collective-permute-start.11 = (bf16[128,5120]{1,0:T(8,128)(2,1)}, bf16[128,5120]{1,0:T(8,128)(2,1)}, u32[]{:S(2)}, u32[]{:S(2)}) collective-permute-start(bf16[128,5120]{1,0:T(8,128)(2,1)} %cut.3.refs_2_), channel_id=1, source_target_pairs={{0,2},{1,3},{2,0},{3,1},{4,6},{5,7},{6,4},{7,5},{8,10},{9,11},{10,... | collective-permute-start | bytes 3932168 | tf_op jit(solution)/shard_map/ppermute | solution.py:547
  103.0 30.9 %collective-permute-start.15 = (bf16[256,1024]{1,0:T(8,128)(2,1)}, bf16[256,1024]{1,0:T(8,128)(2,1)}, u32[]{:S(2)}, u32[]{:S(2)}) collective-permute-start(bf16[256,1024]{1,0:T(8,128)(2,1)} %pick.6.refs_8_), channel_id=1, source_target_pairs={{0,2},{1,3},{2,0},{3,1},{4,6},{5,7},{6,4},{7,5},{8,10},{9,11},{10,... | collective-permute-start | bytes 1572872 | tf_op jit(solution)/shard_map/ppermute | solution.py:547
  133.8 61.8 %collective-permute-start.16 = (bf16[512,1536]{1,0:T(8,128)(2,1)}, bf16[512,1536]{1,0:T(8,128)(2,1)}, u32[]{:S(2)}, u32[]{:S(2)}) collective-permute-start(bf16[512,1536]{1,0:T(8,128)(2,1)} %get-tuple-element.124), channel_id=1, source_target_pairs={{0,1},{1,0},{2,3},{3,2},{4,5},{5,4},{6,7},{7,6},{8,9},{9,8},{10,11... | collective-permute-start | bytes 4718600 | tf_op jit(solution)/shard_map/ppermute | solution.py:547
  195.4 66.6 %collective-permute-start.27 = (bf16[1024,1024]{1,0:T(8,128)(2,1)}, bf16[1024,1024]{1,0:T(8,128)(2,1)}, u32[]{:S(2)}, u32[]{:S(2)}) collective-permute-start(bf16[1024,1024]{1,0:T(8,128)(2,1)} %grad_x.3.refs_5_), channel_id=1, source_target_pairs={{0,2},{1,3},{2,0},{3,1},{4,6},{5,7},{6,4},{7,5},{8,10},{9,11},{10,... | collective-permute-start | bytes 6291464 | tf_op jit(solution)/shard_map/ppermute | solution.py:547
  203.4 94.6 %collective-permute-start.30 = (bf16[1024,1024]{1,0:T(8,128)(2,1)}, bf16[1024,1024]{1,0:T(8,128)(2,1)}, u32[]{:S(2)}, u32[]{:S(2)}) collective-permute-start(bf16[1024,1024]{1,0:T(8,128)(2,1)} %grad_x.4.refs_10_), channel_id=1, source_target_pairs={{0,2},{1,3},{2,0},{3,1},{4,6},{5,7},{6,4},{7,5},{8,10},{9,11},{10,... | collective-permute-start | bytes 6291464 | tf_op jit(solution)/shard_map/ppermute | solution.py:547
  259.0 75.1 %collective-permute-start.29 = (bf16[1024,1024]{1,0:T(8,128)(2,1)}, bf16[1024,1024]{1,0:T(8,128)(2,1)}, u32[]{:S(2)}, u32[]{:S(2)}) collective-permute-start(bf16[1024,1024]{1,0:T(8,128)(2,1)} %grad_x.5.refs_6_), channel_id=1, source_target_pairs={{0,2},{1,3},{2,0},{3,1},{4,6},{5,7},{6,4},{7,5},{8,10},{9,11},{10,... | collective-permute-start | bytes 6291464 | tf_op jit(solution)/shard_map/ppermute | solution.py:547
  269.9 25.1 %collective-permute-start.31 = (bf16[512,1024]{1,0:T(8,128)(2,1)S(1)}, bf16[512,1024]{1,0:T(8,128)(2,1)S(1)}, u32[]{:S(2)}, u32[]{:S(2)}) collective-permute-start(bf16[512,1024]{1,0:T(8,128)(2,1)S(1)} %get-tuple-element.143), channel_id=1, source_target_pairs={{0,4},{4,0},{8,12},{12,8},{16,20},{20,16},{24,28},{28,24},{1,5},{5... | collective-permute-start | bytes 3145736 | tf_op jit(solution)/shard_map/ppermute | solution.py:547
  272.9 92.7 %collective-permute-start.28 = (f32[32,1024]{1,0:T(8,128)}, f32[32,1024]{1,0:T(8,128)}, u32[]{:S(2)}, u32[]{:S(2)}) collective-permute-start(f32[32,1024]{1,0:T(8,128)} %lines_add.5.refs_5_.refs_1_), channel_id=1, source_target_pairs={{0,2},{1,3},{2,0},{3,1},{4,6},{5,7},{6,4},{7,5},{8,10},{9,11},{10,... | collective-permute-start | bytes 393224 | tf_op jit(solution)/shard_map/ppermute | solution.py:547
  305.6 24.3 %collective-permute-start.32 = (bf16[512,1024]{1,0:T(8,128)(2,1)}, bf16[512,1024]{1,0:T(8,128)(2,1)}, u32[]{:S(2)}, u32[]{:S(2)}) collective-permute-start(bf16[512,1024]{1,0:T(8,128)(2,1)} %get-tuple-element.146), channel_id=1, source_target_pairs={{0,4},{4,0},{8,12},{12,8},{16,20},{20,16},{24,28},{28,24},{1,5},{5... | collective-permute-start | bytes 3145736 | tf_op jit(solution)/shard_map/ppermute | solution.py:547
  312.5 34.3 %collective-permute-start.37 = (bf16[256,1024]{1,0:T(8,128)(2,1)}, bf16[256,1024]{1,0:T(8,128)(2,1)}, u32[]{:S(2)}, u32[]{:S(2)}) collective-permute-start(bf16[256,1024]{1,0:T(8,128)(2,1)} %grad_add.8.refs_5_.refs_1_), channel_id=1, source_target_pairs={{0,16},{4,20},{8,24},{12,28},{16,0},{20,4},{24,8},{28,12},{1,17},{... | collective-permute-start | bytes 1572872 | tf_op jit(solution)/shard_map/ppermute | solution.py:547
  349.4 41.4 %collective-permute-start.45 = (bf16[256,1024]{1,0:T(8,128)(2,1)}, bf16[256,1024]{1,0:T(8,128)(2,1)}, u32[]{:S(2)}, u32[]{:S(2)}) collective-permute-start(bf16[256,1024]{1,0:T(8,128)(2,1)} %grad_add.9.refs_3_.refs_1_), channel_id=1, source_target_pairs={{0,8},{4,12},{8,0},{12,4},{16,24},{20,28},{24,16},{28,20},{1,9},{5... | collective-permute-start | bytes 1572872 | tf_op jit(solution)/shard_map/ppermute | solution.py:547
  352.7 41.0 %collective-permute-start.44 = (bf16[256,1024]{1,0:T(8,128)(2,1)}, bf16[256,1024]{1,0:T(8,128)(2,1)}, u32[]{:S(2)}, u32[]{:S(2)}) collective-permute-start(bf16[256,1024]{1,0:T(8,128)(2,1)} %grad_add.10.refs_5_.refs_1_), channel_id=1, source_target_pairs={{0,16},{4,20},{8,24},{12,28},{16,0},{20,4},{24,8},{28,12},{1,17},{... | collective-permute-start | bytes 1572872 | tf_op jit(solution)/shard_map/ppermute | solution.py:547
  357.8 23.3 %collective-permute-start.40 = (bf16[128,1024]{1,0:T(8,128)(2,1)}, bf16[128,1024]{1,0:T(8,128)(2,1)}, u32[]{:S(2)}, u32[]{:S(2)}) collective-permute-start(bf16[128,1024]{1,0:T(8,128)(2,1)} %get-tuple-element.157), channel_id=1, source_target_pairs={{0,8},{4,12},{8,0},{12,4},{16,24},{20,28},{24,16},{28,20},{1,9},{5... | collective-permute-start | bytes 786440 | tf_op jit(solution)/shard_map/ppermute | solution.py:547
  367.8 28.5 %collective-permute-start.43 = (f32[32,1024]{1,0:T(8,128)}, f32[32,1024]{1,0:T(8,128)}, u32[]{:S(2)}, u32[]{:S(2)}) collective-permute-start(f32[32,1024]{1,0:T(8,128)} %lines_add.6.refs_2_.refs_1_), channel_id=1, source_target_pairs={{0,4},{4,0},{8,12},{12,8},{16,20},{20,16},{24,28},{28,24},{1,5},{5... | collective-permute-start | bytes 393224 | tf_op jit(solution)/shard_map/ppermute | solution.py:547
  381.1 28.9 %collective-permute-start.38 = (bf16[256,1024]{1,0:T(8,128)(2,1)}, bf16[256,1024]{1,0:T(8,128)(2,1)}, u32[]{:S(2)}, u32[]{:S(2)}) collective-permute-start(bf16[256,1024]{1,0:T(8,128)(2,1)} %relay.2.refs_3_), channel_id=1, source_target_pairs={{0,2},{1,3},{2,0},{3,1},{4,6},{5,7},{6,4},{7,5},{8,10},{9,11},{10,... | collective-permute-start | bytes 1572872 | tf_op jit(solution)/shard_map/ppermute | solution.py:547
  393.6 42.5 %collective-permute-start.47 = (bf16[512,1024]{1,0:T(8,128)(2,1)}, bf16[512,1024]{1,0:T(8,128)(2,1)}, u32[]{:S(2)}, u32[]{:S(2)}) collective-permute-start(bf16[512,1024]{1,0:T(8,128)(2,1)} %grad_join.4.refs_3_.refs_1_), channel_id=1, source_target_pairs={{0,4},{4,0},{8,12},{12,8},{16,20},{20,16},{24,28},{28,24},{1,5},{5... | collective-permute-start | bytes 3145736 | tf_op jit(solution)/shard_map/ppermute | solution.py:547
  403.3 29.7 %collective-permute-start.48 = (f32[32,1024]{1,0:T(8,128)}, f32[32,1024]{1,0:T(8,128)}, u32[]{:S(2)}, u32[]{:S(2)}) collective-permute-start(f32[32,1024]{1,0:T(8,128)} %lines_add.7.refs_3_.refs_1_), channel_id=1, source_target_pairs={{0,8},{4,12},{8,0},{12,4},{16,24},{20,28},{24,16},{28,20},{1,9},{5... | collective-permute-start | bytes 393224 | tf_op jit(solution)/shard_map/ppermute | solution.py:547
  418.5 24.2 %collective-permute-start.46 = (bf16[256,1024]{1,0:T(8,128)(2,1)}, bf16[256,1024]{1,0:T(8,128)(2,1)}, u32[]{:S(2)}, u32[]{:S(2)}) collective-permute-start(bf16[256,1024]{1,0:T(8,128)(2,1)} %relay.3.refs_3_), channel_id=1, source_target_pairs={{0,2},{1,3},{2,0},{3,1},{4,6},{5,7},{6,4},{7,5},{8,10},{9,11},{10,... | collective-permute-start | bytes 1572872 | tf_op jit(solution)/shard_map/ppermute | solution.py:547
  426.1 26.4 %collective-permute-start.54 = (bf16[512,1024]{1,0:T(8,128)(2,1)}, bf16[512,1024]{1,0:T(8,128)(2,1)}, u32[]{:S(2)}, u32[]{:S(2)}) collective-permute-start(bf16[512,1024]{1,0:T(8,128)(2,1)} %grad_join.5.refs_3_.refs_1_), channel_id=1, source_target_pairs={{0,4},{4,0},{8,12},{12,8},{16,20},{20,16},{24,28},{28,24},{1,5},{5... | collective-permute-start | bytes 3145736 | tf_op jit(solution)/shard_map/ppermute | solution.py:547
  429.5 33.4 %collective-permute-start.52 = (bf16[256,1024]{1,0:T(8,128)(2,1)}, bf16[256,1024]{1,0:T(8,128)(2,1)}, u32[]{:S(2)}, u32[]{:S(2)}) collective-permute-start(bf16[256,1024]{1,0:T(8,128)(2,1)} %grad_join.6.refs_3_.refs_1_), channel_id=1, source_target_pairs={{0,4},{4,0},{8,12},{12,8},{16,20},{20,16},{24,28},{28,24},{1,5},{5... | collective-permute-start | bytes 1572872 | tf_op jit(solution)/shard_map/ppermute | solution.py:547
  433.0 34.7 %collective-permute-start.55 = (bf16[256,1024]{1,0:T(8,128)(2,1)}, bf16[256,1024]{1,0:T(8,128)(2,1)}, u32[]{:S(2)}, u32[]{:S(2)}) collective-permute-start(bf16[256,1024]{1,0:T(8,128)(2,1)} %grad_join.7.refs_3_.refs_1_), channel_id=1, source_target_pairs={{0,4},{4,0},{8,12},{12,8},{16,20},{20,16},{24,28},{28,24},{1,5},{5... | collective-permute-start | bytes 1572872 | tf_op jit(solution)/shard_map/ppermute | solution.py:547
  (60 other events, 586.4 us)
Sparse Core Ops, SparseCore 0:
  38.0 90.8 all-gather.1
where the time goes:
time: 486 us; the launch traced here: 479 us
  Pallas kernels  306 us (63%)
  waiting for transfers between devices  90.2 us (19%)
  starting transfers between devices  48.6 us (10%)
  between operations  16 us (3%)
  local copies, waits for them, and re-layouts  15.4 us (3%)
    pallas_call x62, Pallas kernels, run_kernel(): pl.pallas_call(kernel, grid_spec=pltpu.PrefetchScalarGridSpec(num_scalar_...  306 us
    ppermute x56, waiting for transfers between devices, swap(): return lax.ppermute(value, axis, [(i, i ^ bit) for i in range(size)])  90.2 us
    ppermute x56, starting transfers between devices, swap(): return lax.ppermute(value, axis, [(i, i ^ bit) for i in range(size)])  48.6 us
    unnamed x54, local copies, waits for them, and re-layouts  11.4 us
  transfers between devices with their start and end apart: 57, of which 18 were waited for; matrix products, arithmetic and copies ran while one was open for 1% of the time, Pallas kernels for 63%

commit v1 on v0

--- a/solution.py
+++ b/solution.py
@@ -17,7 +17,7 @@
 ROWS_ROWS = (((0,), (0,)), ((), ()))
 COLS_COLS = (((1,), (1,)), ((), ()))
 ANY = pl.BlockSpec(memory_space=pl.ANY)
-VMEM_MB = dict(grad_z=16,grad_add=16,grad_join=16,lines_add=16,lines=16,relay=16,pair=16,two=16,grad_out=16,grad_y=24)
+VMEM_MB = dict(grad_z=16,grad_add=16,grad_join=16,lines_add=16,lines=16,relay=16,grad_y=24)
 COST = 10**11
 MICROSECONDS = dict(
     pick=2, cut=2, pack=3, split=2, copy=2, relay=2, columns=2, remote=3, key_value=7, query=4, attend=9, output=6,
@@ -873,7 +873,9 @@
         lefts, rights, (lefts_away, lambda b: 2 + 2 * last_one(b)), (lefts_away, lambda b: 3 + 2 * last_one(b)),
         [query_far, key_far, value_far, out_far], lambda shard, b: shard + 4 * last_one(b), lambda b: b,
     )
-    last = grads_four.start(time_sum)
+    down, up = Chunk(grads_down, 0, 4), Chunk(grads_up, 0, 4)
+    last = down.over_y(time_sum)
+    last = grads_four.start(last)
 
     packed = run(
         "lines", lines_kernel, (1,), [whole(a) for a in (down_sums, first_sums, delta_sums, up_sums, time_sum)],
@@ -889,18 +891,17 @@
             line_got.append(swap(line_parts[-1], *hops[len(line_got)]))
         return line_parts[-1]
 
-    down, up = Chunk(grads_down, 0, 4), Chunk(grads_up, 0, 4)
     qk, vo = Chunk(grads_four, 0, 2), Chunk(grads_four, 2, 2)
-    last = down.over_y(packed)
+    last = down.over_z(packed)
     last = add_lines(last)
-    last = down.over_z(last)
     last = up.over_y(last)
     last = down.add_high(last)
     last = up.over_z(last)
+    last = down.add_low(last)
     last = qk.over_y(last)
     last = vo.over_y(last)
-    last = down.add_low(last)
     last = up.add_high(last)
+    last = down.back(last)
     last = qk.over_z(last)
     last = vo.over_z(last)
     last = add_lines(last)
@@ -908,20 +909,19 @@
     final_got = swap_chip(final_away)
     last = qk.add_high(last)
     last = vo.add_high(last)
-    last = down.back(last)
     last = up.add_low(last)
     last = add_lines(last)
+    last = down_grad = down.finish(last, down_weight.shape, lambda s: (s, 0))
     last = qk.add_low(last)
     last = vo.add_low(last)
-    last = final = pair_of(final_mine, final_got, BF16, last)
     last = input_away = relay(input_away, last)
     input_got = swap_chip(input_away)
     last = up.back(last)
+    last = final = pair_of(final_mine, final_got, BF16, last)
     last = qk.back(last)
     last = vo.back(last)
     while len(line_parts) < len(hops):
         last = add_lines(last)
-    last = down_grad = down.finish(last, down_weight.shape, lambda s: (s, 0))
     last = input_gradient = pair_of(input_mine, input_got, F32, last)
     last = up_grad = up.finish(last, up_weight.shape, lambda s: (0, s))
     last = add_lines(last)

time: 486 us -> 477 us (0.981)
  waiting for transfers between devices: 90.2 us -> 81.9 us
  Pallas kernels: 306 us -> 311 us
    ppermute x56, waiting for transfers between devices: 90.2 us -> 81.9 us  [swap(): return lax.ppermute(value, axis, [(i, i ^ bit) for i in range(size)])]
    unnamed x54 -> x68, local copies, waits for them, and re-layouts: 11.4 us -> 11.8 us
  transfers between devices with their start and end apart: 57 -> 57, of which waited for: 18 -> 22; matrix products, arithmetic and copies ran while one was open for 1% -> 1% of each run, Pallas kernels for 63% -> 65%
where the time goes in v1:
time: 477 us; the launch traced here: 472 us
  Pallas kernels  311 us (65%)
  waiting for transfers between devices  81.9 us (17%)
  starting transfers between devices  44.4 us (9%)
  between operations  16.1 us (3%)
  local copies, waits for them, and re-layouts  15.8 us (3%)
    pallas_call x62, Pallas kernels, run_kernel(): pl.pallas_call(kernel, grid_spec=pltpu.PrefetchScalarGridSpec(num_scalar_...  311 us
    ppermute x56, waiting for transfers between devices, swap(): return lax.ppermute(value, axis, [(i, i ^ bit) for i in range(size)])  81.9 us
    ppermute x56, starting transfers between devices, swap(): return lax.ppermute(value, axis, [(i, i ^ bit) for i in range(size)])  44.4 us
    unnamed x68, local copies, waits for them, and re-layouts  11.8 us
  transfers between devices with their start and end apart: 57, of which 22 were waited for; matrix products, arithmetic and copies ran while one was open for 1% of the time, Pallas kernels for 65%

profile of v1, /device:TPU:0, one launch (start us, length us, event | category | flops | bytes accessed | tf_op | source)
XLA Modules:
  0.0 471.8 jit_solution(11783681534782867282)
XLA Ops:
  37.9 6.2 %collective-permute-done.refs_1_ = bf16[128,3072]{1,0:T(8,128)(2,1)} collective-permute-done((bf16[128,3072]{1,0:T(8,128)(2,1)}, bf16[128,3072]{1,0:T(8,128)(2,1)}, u32[]{:S(2)}, u32[]{:S(2)}) %collective-permute-start) | collective-permute-done | bytes 786464 | tf_op jit(solution)/shard_map/ppermute | solution.py:547
  64.0 8.6 %key_value.1 = (bf16[512,1024]{1,0:T(8,128)(2,1)}, bf16[512,1024]{1,0:T(8,128)(2,1)}, bf16[1024,3072]{1,0:T(8,128)(2,1)}, bf16[512,2048]{1,0:T(8,128)(2,1)}) custom-call(s32[4]{0:T(128)} %pad_add_fusion.refs_0_, bf16[256,1024]{1,0:T(8,128)(2,1)} %pick.5.refs_4_.refs_1_.refs_3_, bf16[272,1024]{1,0:T(8,128)(2,1)} %collective-permute-done.3.refs_3_.refs_2_.refs_4_, ...), custom_call_target="tpu_custom_call" | custom-call | flops 699999977472 | tf_op jit(solution)/shard_map/key_value/pallas_call | solution.py:44
  78.1 10.8 %attend.2 = (bf16[512,2048]{1,0:T(8,128)(2,1)}, f32[4,4,512]{2,1,0:T(4,128)}) custom-call(s32[4]{0:T(128)} %pad_add_fusion.refs_0_, bf16[512,1024]{1,0:T(8,128)(2,1)} %get-tuple-element.100.refs_1_, bf16[512,1024]{1,0:T(8,128)(2,1)} %get-tuple-element.101.refs_2_, bf16[512,1024]{1,0:T(8,128)(2,1)} %get-tuple-element.102.refs_3_, ...), custom_call_target="tpu_custom_call", output_to_operand_aliasing={{0}: (6, {})} | custom-call | flops 899999989760 | tf_op jit(solution)/shard_map/attend/pallas_call | solution.py:44
  88.9 5.5 %collective-permute-done.11.refs_1_ = bf16[128,5120]{1,0:T(8,128)(2,1)} collective-permute-done((bf16[128,5120]{1,0:T(8,128)(2,1)}, bf16[128,5120]{1,0:T(8,128)(2,1)}, u32[]{:S(2)}, u32[]{:S(2)}) %collective-permute-start.11) | collective-permute-done | bytes 1310752 | tf_op jit(solution)/shard_map/ppermute | solution.py:547
  105.5 11.4 %attend.3 = (bf16[512,2048]{1,0:T(8,128)(2,1)}, f32[4,4,512]{2,1,0:T(4,128)}) custom-call(s32[4]{0:T(128)} %pad_add_fusion.refs_0_, bf16[512,1024]{1,0:T(8,128)(2,1)} %get-tuple-element.100.refs_1_, bf16[512,1024]{1,0:T(8,128)(2,1)} %get-tuple-element.101.refs_2_, ...), custom_call_target="tpu_custom_call", output_to_operand_aliasing={{0}: (6, {}), {1}: (7, {})} | custom-call | flops 899999989760 | tf_op jit(solution)/shard_map/attend/pallas_call | solution.py:44
  126.2 7.6 %output.1 = (bf16[1024,1024]{1,0:T(8,128)(2,1)}, f32[512,1024]{1,0:T(8,128)}, f32[512,1]{1,0:T(8,128)}, bf16[512,1024]{1,0:T(8,128)(2,1)}, bf16[512,1536]{1,0:T(8,128)(2,1)}) custom-call(s32[4]{0:T(128)} %pad_add_fusion.refs_0_, bf16[512,2048]{1,0:T(8,128)(2,1)} %get-tuple-element.106.refs_1_.refs_2_, bf16[512,2048]{1,0:T(8,128)(2,1)} %get-tuple-element.106.refs_1_.refs_2_, ...), custom_call_target="tpu_custom_call" | custom-call | flops 599999971328 | tf_op jit(solution)/shard_map/output/pallas_call | solution.py:44
  134.0 42.8 %feed_forward.1 = (bf16[512,4096]{1,0:T(8,128)(2,1)}, bf16[512,2048]{1,0:T(8,128)(2,1)}, bf16[256,1024]{1,0:T(8,128)(2,1)}, bf16[256,1024]{1,0:T(8,128)(2,1)}, b...) custom-call(s32[4]{0:T(128)} %pad_add_fusion.refs_0_, ...), custom_call_target="tpu_custom_call" | custom-call | flops 3999999983616 | tf_op jit(solution)/shard_map/feed_forward/pallas_call | solution.py:44
  177.8 10.2 %attend_back.2 = (bf16[512,1024]{1,0:T(8,128)(2,1)}, bf16[512,4096]{1,0:T(8,128)(2,1)}, f32[512,512]{1,0:T(8,128)}, bf16[512,512]{1,0:T(8,128)(2,1)}) custom-call(s32[4]{0:T(128)} %pad_add_fusion.refs_0_, bf16[512,1024]{1,0:T(8,128)(2,1)} %get-tuple-element.100.refs_1_, ...), custom_call_target="tpu_custom_call", output_to_operand_aliasing={{1}: (8, {})} | custom-call | flops 1500000026624 | tf_op jit(solution)/shard_map/attend_back/pallas_call | solution.py:44
  188.4 7.3 %grad_x.3.refs_5_ = bf16[1024,1024]{1,0:T(8,128)(2,1)} custom-call(s32[4]{0:T(128)} %pad_add_fusion.refs_0_, bf16[512,4096]{1,0:T(8,128)(2,1)} %get-tuple-element.125.refs_1_, bf16[512,1024]{1,0:T(8,128)(2,1)} %get-tuple-element.126.refs_2_, bf16[512,2048]{1,0:T(8,128)(2,1)} %collective-permute-done.18.refs_3_, ...), custom_call_target="tpu_custom_call" | custom-call | flops 799999983616 | tf_op jit(solution)/shard_map/grad_x/pallas_call | solution.py:44
  195.8 7.8 %grad_x.4.refs_10_ = bf16[1024,1024]{1,0:T(8,128)(2,1)} custom-call(s32[4]{0:T(128)} %pad_add_fusion.refs_0_, bf16[512,1024]{1,0:T(8,128)(2,1)} %get-tuple-element.109.refs_1_, bf16[512,4096]{1,0:T(8,128)(2,1)} %get-tuple-element.123.refs_2_, bf16[512,1536]{1,0:T(8,128)(2,1)} %collective-permute-done.16.refs_3_, ...), custom_call_target="tpu_custom_call" | custom-call | flops 799999983616 | tf_op jit(solution)/shard_map/grad_x/pallas_call | solution.py:44
  205.5 23.9 %attend_back.3 = (bf16[512,1024]{1,0:T(8,128)(2,1)}, bf16[512,4096]{1,0:T(8,128)(2,1)}, f32[512,1536]{1,0:T(8,128)}, bf16[512,1536]{1,0:T(8,128)(2,1)}) custom-call(s32[4]{0:T(128)} %pad_add_fusion.refs_0_, bf16[512,1024]{1,0:T(8,128)(2,1)} %get-tuple-element.100.refs_1_, ...), custom_call_target="tpu_custom_call", output_to_operand_aliasing={{1}: (8, {}), {0}: (9, {})} | custom-call | flops 1500000026624 | tf_op jit(solution)/shard_map/attend_back/pallas_call | solution.py:44
  235.2 6.7 %delta.1 = (bf16[512,1024]{1,0:T(8,128)(2,1)}, bf16[512,1024]{1,0:T(8,128)(2,1)}, bf16[512,4096]{1,0:T(8,128)(2,1)}, f32[8,1024]{1,0:T(8,128)}) custom-call(s32[4]{0:T(128)} %pad_add_fusion.refs_0_, f32[512,512]{1,0:T(8,128)} %get-tuple-element.120.refs_5_.refs_1_, ...), custom_call_target="tpu_custom_call", output_to_operand_aliasing={{2}: (10, {})} | custom-call | flops 499999997952 | tf_op jit(solution)/shard_map/delta/pallas_call | solution.py:44
  242.5 7.7 %input.1 = (f32[256,1024]{1,0:T(8,128)}, bf16[256,1024]{1,0:T(8,128)(2,1)}, f32[1,1024]{1,0:T(1,128)}) custom-call(s32[4]{0:T(128)} %pad_add_fusion.refs_0_, bf16[512,4096]{1,0:T(8,128)(2,1)} %get-tuple-element.138.refs_1_.refs_2_, bf16[1024,3072]{1,0:T(8,128)(2,1)} %get-tuple-element.134.refs_2_, f32[512,1024]{1,0:T(8,128)} %input_query.1.refs_11_.refs_3_, ...), custom_call_target="tpu_custom_call" | custom-call | flops 799999983616 | tf_op jit(solution)/shard_map/input/pallas_call | solution.py:44
  253.1 7.2 %grad_y.4 = (bf16[512,1024]{1,0:T(8,128)(2,1)}, bf16[512,1024]{1,0:T(8,128)(2,1)S(1)}) custom-call(s32[4]{0:T(128)S(1)} %copy-done.2, bf16[512,4096]{1,0:T(8,128)(2,1)S(1)} %copy-done.16, bf16[512,1024]{1,0:T(8,128)(2,1)S(1)} %copy-done.9, bf16[512,2048]{1,0:T(8,128)(2,1)} %collective-permute-done.18.refs_3_, ...), custom_call_target="tpu_custom_call" | custom-call | flops 499999997952 | tf_op jit(solution)/shard_map/grad_y/pallas_call | solution.py:44
  261.7 9.3 %grad_x.5.refs_6_ = bf16[1024,1024]{1,0:T(8,128)(2,1)} custom-call(s32[4]{0:T(128)} %pad_add_fusion.refs_0_, bf16[512,2048]{1,0:T(8,128)(2,1)} %get-tuple-element.106.refs_1_.refs_2_, bf16[512,4096]{1,0:T(8,128)(2,1)} %get-tuple-element.138.refs_1_.refs_2_, bf16[512,1536]{1,0:T(8,128)(2,1)} %collective-permute-done.16.refs_3_, ...), custom_call_target="tpu_custom_call" | custom-call | flops 799999983616 | tf_op jit(solution)/shard_map/grad_x/pallas_call | solution.py:44
  274.5 12.3 %collective-permute-done.28.refs_2_.refs_4_ = bf16[512,1024]{1,0:T(8,128)(2,1)} collective-permute-done((bf16[512,1024]{1,0:T(8,128)(2,1)}, bf16[512,1024]{1,0:T(8,128)(2,1)}, u32[]{:S(2)}, u32[]{:S(2)}) %collective-permute-start.28) | collective-permute-done | bytes 1048608 | tf_op jit(solution)/shard_map/ppermute | solution.py:547
  293.5 7.5 %grad_y.5 = (bf16[512,1024]{1,0:T(8,128)(2,1)}, bf16[512,1024]{1,0:T(8,128)(2,1)S(1)}) custom-call(s32[4]{0:T(128)S(1)} %copy-done.3, bf16[512,1024]{1,0:T(8,128)(2,1)S(1)} %copy-done.24, bf16[512,4096]{1,0:T(8,128)(2,1)S(1)} %copy-done.7, bf16[512,1536]{1,0:T(8,128)(2,1)} %collective-permute-done.16.refs_3_, ...), custom_call_target="tpu_custom_call" | custom-call | flops 499999997952 | tf_op jit(solution)/shard_map/grad_y/pallas_call | solution.py:44
  308.1 17.0 %collective-permute-done.34.refs_2_.refs_4_ = bf16[512,1024]{1,0:T(8,128)(2,1)} collective-permute-done((bf16[512,1024]{1,0:T(8,128)(2,1)}, bf16[512,1024]{1,0:T(8,128)(2,1)}, u32[]{:S(2)}, u32[]{:S(2)}) %collective-permute-start.34) | collective-permute-done | bytes 1048608 | tf_op jit(solution)/shard_map/ppermute | solution.py:547
  334.3 5.3 %grad_y.6 = (bf16[256,1024]{1,0:T(8,128)(2,1)}, bf16[256,1024]{1,0:T(8,128)(2,1)S(1)}) custom-call(s32[4]{0:T(128)S(1)} %copy-done.3, bf16[512,2048]{1,0:T(8,128)(2,1)S(1)} %copy-done.17, bf16[512,4096]{1,0:T(8,128)(2,1)S(1)} %copy-done.15, bf16[512,1536]{1,0:T(8,128)(2,1)} %collective-permute-done.16.refs_3_, ...), custom_call_target="tpu_custom_call" | custom-call | flops 499999997952 | tf_op jit(solution)/shard_map/grad_y/pallas_call | solution.py:44
  340.0 5.3 %grad_y.7 = (bf16[256,1024]{1,0:T(8,128)(2,1)}, bf16[256,1024]{1,0:T(8,128)(2,1)S(1)}) custom-call(s32[4]{0:T(128)S(1)} %copy-done.3, bf16[512,2048]{1,0:T(8,128)(2,1)S(1)} %copy-done.17, bf16[512,4096]{1,0:T(8,128)(2,1)S(1)} %copy-done.15, bf16[512,1536]{1,0:T(8,128)(2,1)} %collective-permute-done.16.refs_3_, ...), custom_call_target="tpu_custom_call" | custom-call | flops 499999997952 | tf_op jit(solution)/shard_map/grad_y/pallas_call | solution.py:44
  359.8 6.2 %collective-permute-done.35.refs_2_.refs_4_ = bf16[256,1024]{1,0:T(8,128)(2,1)} collective-permute-done((bf16[256,1024]{1,0:T(8,128)(2,1)}, bf16[256,1024]{1,0:T(8,128)(2,1)}, u32[]{:S(2)}, u32[]{:S(2)}) %collective-permute-start.35) | collective-permute-done | bytes 524320 | tf_op jit(solution)/shard_map/ppermute | solution.py:547
  393.6 5.3 %grad_out.2.refs_3_ = f32[1024,1024]{1,0:T(8,128)} custom-call(s32[4]{0:T(128)} %pad_add_fusion.refs_0_, bf16[512,1024]{1,0:T(8,128)(2,1)} %grad_join.4.refs_5_.refs_1_, bf16[512,1024]{1,0:T(8,128)(2,1)} %collective-permute-done.46.refs_2_, f32[32,1024]{1,0:T(8,128)} %lines_add.7.refs_3_.refs_1_), custom_call_target="tpu_custom_call" | custom-call | flops 299999985664 | tf_op jit(solution)/shard_map/grad_out/pallas_call | solution.py:44
  437.7 6.6 %collective-permute-done.54.refs_2_ = bf16[512,1024]{1,0:T(8,128)(2,1)} collective-permute-done((bf16[512,1024]{1,0:T(8,128)(2,1)}, bf16[512,1024]{1,0:T(8,128)(2,1)}, u32[]{:S(2)}, u32[]{:S(2)}) %collective-permute-start.54) | collective-permute-done | bytes 1048608 | tf_op jit(solution)/shard_map/ppermute | solution.py:547
  444.3 5.3 %grad_out.3.refs_3_ = f32[256,4096]{1,0:T(8,128)} custom-call(s32[4]{0:T(128)} %pad_add_fusion.refs_0_, bf16[512,1024]{1,0:T(8,128)(2,1)} %grad_join.5.refs_3_.refs_1_, bf16[512,1024]{1,0:T(8,128)(2,1)} %collective-permute-done.54.refs_2_, f32[2,256,1024]{2,1,0:T(8,128)} %pair.3.refs_3_), custom_call_target="tpu_custom_call" | custom-call | flops 299999985664 | tf_op jit(solution)/shard_map/grad_out/pallas_call | solution.py:44
  (235 shorter events, 211.9 us)
Async XLA Ops:
  7.2 126.8 %all-gather.2.cloned.1.call-start = ((), (), s32[]{:S(2)}) async-start(), calls=%async_computation | async-start | bytes 10485760 | tf_op jit(solution)/shard_map/all_gather | solution.py:603
  16.2 27.9 %collective-permute-start = (bf16[128,3072]{1,0:T(8,128)(2,1)}, bf16[128,3072]{1,0:T(8,128)(2,1)}, u32[]{:S(2)}, u32[]{:S(2)}) collective-permute-start(bf16[128,3072]{1,0:T(8,128)(2,1)} %cut.2.refs_4_), channel_id=1, source_target_pairs={{0,2},{1,3},{2,0},{3,1},{4,6},{5,7},{6,4},{7,5},{8,10},{9,11},{10,... | collective-permute-start | bytes 2359304 | tf_op jit(solution)/shard_map/ppermute | solution.py:547
  19.4 24.6 %collective-permute-start.1 = (bf16[256,3072]{1,0:T(8,128)(2,1)}, bf16[256,3072]{1,0:T(8,128)(2,1)}, u32[]{:S(2)}, u32[]{:S(2)}) collective-permute-start(bf16[256,3072]{1,0:T(8,128)(2,1)} %pack.2.refs_3_.refs_4_), channel_id=1, source_target_pairs={{0,1},{1,0},{2,3},{3,2},{4,5},{5,4},{6,7},{7,6},{8,9},{9,8},{10,11... | collective-permute-start | bytes 4718600 | tf_op jit(solution)/shard_map/ppermute | solution.py:547
  32.1 62.3 %collective-permute-start.11 = (bf16[128,5120]{1,0:T(8,128)(2,1)}, bf16[128,5120]{1,0:T(8,128)(2,1)}, u32[]{:S(2)}, u32[]{:S(2)}) collective-permute-start(bf16[128,5120]{1,0:T(8,128)(2,1)} %cut.3.refs_2_), channel_id=1, source_target_pairs={{0,2},{1,3},{2,0},{3,1},{4,6},{5,7},{6,4},{7,5},{8,10},{9,11},{10,... | collective-permute-start | bytes 3932168 | tf_op jit(solution)/shard_map/ppermute | solution.py:547
  103.1 30.9 %collective-permute-start.15 = (bf16[256,1024]{1,0:T(8,128)(2,1)}, bf16[256,1024]{1,0:T(8,128)(2,1)}, u32[]{:S(2)}, u32[]{:S(2)}) collective-permute-start(bf16[256,1024]{1,0:T(8,128)(2,1)} %pick.6.refs_8_), channel_id=1, source_target_pairs={{0,2},{1,3},{2,0},{3,1},{4,6},{5,7},{6,4},{7,5},{8,10},{9,11},{10,... | collective-permute-start | bytes 1572872 | tf_op jit(solution)/shard_map/ppermute | solution.py:547
  133.8 62.0 %collective-permute-start.16 = (bf16[512,1536]{1,0:T(8,128)(2,1)}, bf16[512,1536]{1,0:T(8,128)(2,1)}, u32[]{:S(2)}, u32[]{:S(2)}) collective-permute-start(bf16[512,1536]{1,0:T(8,128)(2,1)} %get-tuple-element.124), channel_id=1, source_target_pairs={{0,1},{1,0},{2,3},{3,2},{4,5},{5,4},{6,7},{7,6},{8,9},{9,8},{10,11... | collective-permute-start | bytes 4718600 | tf_op jit(solution)/shard_map/ppermute | solution.py:547
  195.7 54.6 %collective-permute-start.26 = (bf16[1024,1024]{1,0:T(8,128)(2,1)}, bf16[1024,1024]{1,0:T(8,128)(2,1)}, u32[]{:S(2)}, u32[]{:S(2)}) collective-permute-start(bf16[1024,1024]{1,0:T(8,128)(2,1)} %grad_x.3.refs_5_), channel_id=1, source_target_pairs={{0,2},{1,3},{2,0},{3,1},{4,6},{5,7},{6,4},{7,5},{8,10},{9,11},{10,... | collective-permute-start | bytes 6291464 | tf_op jit(solution)/shard_map/ppermute | solution.py:547
  203.7 89.8 %collective-permute-start.32 = (bf16[1024,1024]{1,0:T(8,128)(2,1)}, bf16[1024,1024]{1,0:T(8,128)(2,1)}, u32[]{:S(2)}, u32[]{:S(2)}) collective-permute-start(bf16[1024,1024]{1,0:T(8,128)(2,1)} %grad_x.4.refs_10_), channel_id=1, source_target_pairs={{0,2},{1,3},{2,0},{3,1},{4,6},{5,7},{6,4},{7,5},{8,10},{9,11},{10,... | collective-permute-start | bytes 6291464 | tf_op jit(solution)/shard_map/ppermute | solution.py:547
  229.5 32.2 %collective-permute-start.23 = (bf16[512,1024]{1,0:T(8,128)(2,1)}, bf16[512,1024]{1,0:T(8,128)(2,1)}, u32[]{:S(2)}, u32[]{:S(2)}) collective-permute-start(bf16[512,1024]{1,0:T(8,128)(2,1)} %get-tuple-element.132.refs_1_.refs_9_), channel_id=1, source_target_pairs={{0,1},{1,0},{2,3},{3,2},{4,5},{5,4},{6,7},{7,6},{8,9},{9,8},{10,11... | collective-permute-start | bytes 3145736 | tf_op jit(solution)/shard_map/ppermute | solution.py:547
  261.3 25.5 %collective-permute-start.28 = (bf16[512,1024]{1,0:T(8,128)(2,1)}, bf16[512,1024]{1,0:T(8,128)(2,1)}, u32[]{:S(2)}, u32[]{:S(2)}) collective-permute-start(bf16[512,1024]{1,0:T(8,128)(2,1)} %get-tuple-element.143), channel_id=1, source_target_pairs={{0,4},{4,0},{8,12},{12,8},{16,20},{20,16},{24,28},{28,24},{1,5},{5... | collective-permute-start | bytes 3145736 | tf_op jit(solution)/shard_map/ppermute | solution.py:547
  271.0 63.3 %collective-permute-start.30 = (bf16[1024,1024]{1,0:T(8,128)(2,1)}, bf16[1024,1024]{1,0:T(8,128)(2,1)}, u32[]{:S(2)}, u32[]{:S(2)}) collective-permute-start(bf16[1024,1024]{1,0:T(8,128)(2,1)} %grad_x.5.refs_6_), channel_id=1, source_target_pairs={{0,2},{1,3},{2,0},{3,1},{4,6},{5,7},{6,4},{7,5},{8,10},{9,11},{10,... | collective-permute-start | bytes 6291464 | tf_op jit(solution)/shard_map/ppermute | solution.py:547
  292.4 76.0 %collective-permute-start.29 = (f32[32,1024]{1,0:T(8,128)}, f32[32,1024]{1,0:T(8,128)}, u32[]{:S(2)}, u32[]{:S(2)}) collective-permute-start(f32[32,1024]{1,0:T(8,128)} %lines_add.5.refs_6_.refs_1_), channel_id=1, source_target_pairs={{0,2},{1,3},{2,0},{3,1},{4,6},{5,7},{6,4},{7,5},{8,10},{9,11},{10,... | collective-permute-start | bytes 393224 | tf_op jit(solution)/shard_map/ppermute | solution.py:547
  301.0 24.1 %collective-permute-start.34 = (bf16[512,1024]{1,0:T(8,128)(2,1)}, bf16[512,1024]{1,0:T(8,128)(2,1)}, u32[]{:S(2)}, u32[]{:S(2)}) collective-permute-start(bf16[512,1024]{1,0:T(8,128)(2,1)} %get-tuple-element.147), channel_id=1, source_target_pairs={{0,4},{4,0},{8,12},{12,8},{16,20},{20,16},{24,28},{28,24},{1,5},{5... | collective-permute-start | bytes 3145736 | tf_op jit(solution)/shard_map/ppermute | solution.py:547
  305.3 24.7 %collective-permute-start.33 = (bf16[256,1024]{1,0:T(8,128)(2,1)}, bf16[256,1024]{1,0:T(8,128)(2,1)}, u32[]{:S(2)}, u32[]{:S(2)}) collective-permute-start(bf16[256,1024]{1,0:T(8,128)(2,1)} %grad_add.8.refs_5_.refs_1_), channel_id=1, source_target_pairs={{0,16},{4,20},{8,24},{12,28},{16,0},{20,4},{24,8},{28,12},{1,17},{... | collective-permute-start | bytes 1572872 | tf_op jit(solution)/shard_map/ppermute | solution.py:547
  332.9 21.1 %collective-permute-start.37 = (bf16[256,1024]{1,0:T(8,128)(2,1)}, bf16[256,1024]{1,0:T(8,128)(2,1)}, u32[]{:S(2)}, u32[]{:S(2)}) collective-permute-start(bf16[256,1024]{1,0:T(8,128)(2,1)} %grad_add.9.refs_7_.refs_1_), channel_id=1, source_target_pairs={{0,8},{4,12},{8,0},{12,4},{16,24},{20,28},{24,16},{28,20},{1,9},{5... | collective-permute-start | bytes 1572872 | tf_op jit(solution)/shard_map/ppermute | solution.py:547
  349.5 34.5 %collective-permute-start.40 = (bf16[256,1024]{1,0:T(8,128)(2,1)}, bf16[256,1024]{1,0:T(8,128)(2,1)}, u32[]{:S(2)}, u32[]{:S(2)}) collective-permute-start(bf16[256,1024]{1,0:T(8,128)(2,1)} %grad_add.10.refs_3_.refs_1_), channel_id=1, source_target_pairs={{0,16},{4,20},{8,24},{12,28},{16,0},{20,4},{24,8},{28,12},{1,17},{... | collective-permute-start | bytes 1572872 | tf_op jit(solution)/shard_map/ppermute | solution.py:547
  356.8 36.0 %collective-permute-start.46 = (bf16[512,1024]{1,0:T(8,128)(2,1)}, bf16[512,1024]{1,0:T(8,128)(2,1)}, u32[]{:S(2)}, u32[]{:S(2)}) collective-permute-start(bf16[512,1024]{1,0:T(8,128)(2,1)} %grad_join.4.refs_5_.refs_1_), channel_id=1, source_target_pairs={{0,4},{4,0},{8,12},{12,8},{16,20},{20,16},{24,28},{28,24},{1,5},{5... | collective-permute-start | bytes 3145736 | tf_op jit(solution)/shard_map/ppermute | solution.py:547
  377.5 40.3 %collective-permute-start.39 = (bf16[256,1024]{1,0:T(8,128)(2,1)}, bf16[256,1024]{1,0:T(8,128)(2,1)}, u32[]{:S(2)}, u32[]{:S(2)}) collective-permute-start(bf16[256,1024]{1,0:T(8,128)(2,1)} %relay.2.refs_3_), channel_id=1, source_target_pairs={{0,2},{1,3},{2,0},{3,1},{4,6},{5,7},{6,4},{7,5},{8,10},{9,11},{10,... | collective-permute-start | bytes 1572872 | tf_op jit(solution)/shard_map/ppermute | solution.py:547
  384.0 21.3 %collective-permute-start.44 = (bf16[128,1024]{1,0:T(8,128)(2,1)}, bf16[128,1024]{1,0:T(8,128)(2,1)}, u32[]{:S(2)}, u32[]{:S(2)}) collective-permute-start(bf16[128,1024]{1,0:T(8,128)(2,1)} %grad_add.12.refs_3_.refs_1_), channel_id=1, source_target_pairs={{0,16},{4,20},{8,24},{12,28},{16,0},{20,4},{24,8},{28,12},{1,17},{... | collective-permute-start | bytes 786440 | tf_op jit(solution)/shard_map/ppermute | solution.py:547
  389.3 25.7 %collective-permute-start.43 = (bf16[256,1024]{1,0:T(8,128)(2,1)}, bf16[256,1024]{1,0:T(8,128)(2,1)}, u32[]{:S(2)}, u32[]{:S(2)}) collective-permute-start(bf16[256,1024]{1,0:T(8,128)(2,1)} %grad_add.13.refs_3_.refs_1_), channel_id=1, source_target_pairs={{0,8},{4,12},{8,0},{12,4},{16,24},{20,28},{24,16},{28,20},{1,9},{5... | collective-permute-start | bytes 1572872 | tf_op jit(solution)/shard_map/ppermute | solution.py:547
  392.7 38.8 %collective-permute-start.49 = (f32[32,1024]{1,0:T(8,128)}, f32[32,1024]{1,0:T(8,128)}, u32[]{:S(2)}, u32[]{:S(2)}) collective-permute-start(f32[32,1024]{1,0:T(8,128)} %lines_add.7.refs_3_.refs_1_), channel_id=1, source_target_pairs={{0,8},{4,12},{8,0},{12,4},{16,24},{20,28},{24,16},{28,20},{1,9},{5... | collective-permute-start | bytes 393224 | tf_op jit(solution)/shard_map/ppermute | solution.py:547
  417.9 26.4 %collective-permute-start.54 = (bf16[512,1024]{1,0:T(8,128)(2,1)}, bf16[512,1024]{1,0:T(8,128)(2,1)}, u32[]{:S(2)}, u32[]{:S(2)}) collective-permute-start(bf16[512,1024]{1,0:T(8,128)(2,1)} %grad_join.5.refs_3_.refs_1_), channel_id=1, source_target_pairs={{0,4},{4,0},{8,12},{12,8},{16,20},{20,16},{24,28},{28,24},{1,5},{5... | collective-permute-start | bytes 3145736 | tf_op jit(solution)/shard_map/ppermute | solution.py:547
  427.1 28.4 %collective-permute-start.52 = (bf16[256,1024]{1,0:T(8,128)(2,1)}, bf16[256,1024]{1,0:T(8,128)(2,1)}, u32[]{:S(2)}, u32[]{:S(2)}) collective-permute-start(bf16[256,1024]{1,0:T(8,128)(2,1)} %grad_join.6.refs_3_.refs_1_), channel_id=1, source_target_pairs={{0,4},{4,0},{8,12},{12,8},{16,20},{20,16},{24,28},{28,24},{1,5},{5... | collective-permute-start | bytes 1572872 | tf_op jit(solution)/shard_map/ppermute | solution.py:547
  430.0 31.3 %collective-permute-start.55 = (bf16[256,1024]{1,0:T(8,128)(2,1)}, bf16[256,1024]{1,0:T(8,128)(2,1)}, u32[]{:S(2)}, u32[]{:S(2)}) collective-permute-start(bf16[256,1024]{1,0:T(8,128)(2,1)} %grad_join.7.refs_3_.refs_1_), channel_id=1, source_target_pairs={{0,4},{4,0},{8,12},{12,8},{16,20},{20,16},{24,28},{28,24},{1,5},{5... | collective-permute-start | bytes 1572872 | tf_op jit(solution)/shard_map/ppermute | solution.py:547
  (68 other events, 668.6 us)
Sparse Core Ops, SparseCore 0:
  38.0 90.8 all-gather.1

commit v2 on v1

--- a/solution.py
+++ b/solution.py
@@ -902,28 +902,28 @@
     last = vo.over_y(last)
     last = up.add_high(last)
     last = down.back(last)
+    last = add_lines(last)
     last = qk.over_z(last)
     last = vo.over_z(last)
-    last = add_lines(last)
     last = final_away = relay(final_away, last)
     final_got = swap_chip(final_away)
+    last = up.add_low(last)
     last = qk.add_high(last)
     last = vo.add_high(last)
-    last = up.add_low(last)
     last = add_lines(last)
     last = down_grad = down.finish(last, down_weight.shape, lambda s: (s, 0))
+    last = up.back(last)
     last = qk.add_low(last)
     last = vo.add_low(last)
     last = input_away = relay(input_away, last)
     input_got = swap_chip(input_away)
-    last = up.back(last)
     last = final = pair_of(final_mine, final_got, BF16, last)
     last = qk.back(last)
     last = vo.back(last)
     while len(line_parts) < len(hops):
         last = add_lines(last)
+    last = up_grad = up.finish(last, up_weight.shape, lambda s: (0, s))
     last = input_gradient = pair_of(input_mine, input_got, F32, last)
-    last = up_grad = up.finish(last, up_weight.shape, lambda s: (0, s))
     last = add_lines(last)
 
     def two(chunk, last):

time: 477 us -> 469 us (0.983)
  waiting for transfers between devices: 81.9 us -> 74 us
    ppermute x56, waiting for transfers between devices: 81.9 us -> 74 us  [swap(): return lax.ppermute(value, axis, [(i, i ^ bit) for i in range(size)])]
    unnamed x68 -> x76, local copies, waits for them, and re-layouts: 11.8 us -> 11.2 us
  transfers between devices with their start and end apart: 57 -> 57, of which waited for: 22 -> 20; matrix products, arithmetic and copies ran while one was open for 1% -> 1% of each run, Pallas kernels for 65% -> 66%
where the time goes in v2:
time: 469 us; the launch traced here: 464 us
  Pallas kernels  311 us (66%)
  waiting for transfers between devices  74 us (16%)
  starting transfers between devices  45.4 us (10%)
  between operations  16.1 us (3%)
  local copies, waits for them, and re-layouts  15.2 us (3%)
    pallas_call x62, Pallas kernels, run_kernel(): pl.pallas_call(kernel, grid_spec=pltpu.PrefetchScalarGridSpec(num_scalar_...  311 us
    ppermute x56, waiting for transfers between devices, swap(): return lax.ppermute(value, axis, [(i, i ^ bit) for i in range(size)])  74 us
    ppermute x56, starting transfers between devices, swap(): return lax.ppermute(value, axis, [(i, i ^ bit) for i in range(size)])  45.3 us
    unnamed x76, local copies, waits for them, and re-layouts  11.2 us
  transfers between devices with their start and end apart: 57, of which 20 were waited for; matrix products, arithmetic and copies ran while one was open for 1% of the time, Pallas kernels for 66%

profile of v2, /device:TPU:0, one launch (start us, length us, event | category | flops | bytes accessed | tf_op | source)
XLA Modules:
  0.0 464.2 jit_solution(11316809811643148950)
XLA Ops:
  37.9 6.2 %collective-permute-done.refs_1_ = bf16[128,3072]{1,0:T(8,128)(2,1)} collective-permute-done((bf16[128,3072]{1,0:T(8,128)(2,1)}, bf16[128,3072]{1,0:T(8,128)(2,1)}, u32[]{:S(2)}, u32[]{:S(2)}) %collective-permute-start) | collective-permute-done | bytes 786464 | tf_op jit(solution)/shard_map/ppermute | solution.py:547
  64.0 8.6 %key_value.1 = (bf16[512,1024]{1,0:T(8,128)(2,1)}, bf16[512,1024]{1,0:T(8,128)(2,1)}, bf16[1024,3072]{1,0:T(8,128)(2,1)}, bf16[512,2048]{1,0:T(8,128)(2,1)}) custom-call(s32[4]{0:T(128)} %pad_add_fusion.refs_0_, bf16[256,1024]{1,0:T(8,128)(2,1)} %pick.5.refs_4_.refs_1_.refs_3_, bf16[272,1024]{1,0:T(8,128)(2,1)} %collective-permute-done.3.refs_3_.refs_2_.refs_4_, ...), custom_call_target="tpu_custom_call" | custom-call | flops 699999977472 | tf_op jit(solution)/shard_map/key_value/pallas_call | solution.py:44
  73.2 4.9 %query.1 = (bf16[512,1024]{1,0:T(8,128)(2,1)}, bf16[1024,3072]{1,0:T(8,128)(2,1)}) custom-call(s32[4]{0:T(128)} %pad_add_fusion.refs_0_, bf16[512,2048]{1,0:T(8,128)(2,1)} %get-tuple-element.97.refs_1_.refs_6_, f32[16,1024]{1,0:T(8,128)} %get-tuple-element.96.refs_3_.refs_2_.refs_5_.refs_7_, ...), custom_call_target="tpu_custom_call", output_to_operand_aliasing={{1}: (7, {})} | custom-call | flops 399999991808 | tf_op jit(solution)/shard_map/query/pallas_call | solution.py:44
  78.2 10.8 %attend.2 = (bf16[512,2048]{1,0:T(8,128)(2,1)}, f32[4,4,512]{2,1,0:T(4,128)}) custom-call(s32[4]{0:T(128)} %pad_add_fusion.refs_0_, bf16[512,1024]{1,0:T(8,128)(2,1)} %get-tuple-element.100.refs_1_, bf16[512,1024]{1,0:T(8,128)(2,1)} %get-tuple-element.101.refs_2_, bf16[512,1024]{1,0:T(8,128)(2,1)} %get-tuple-element.102.refs_3_, ...), custom_call_target="tpu_custom_call", output_to_operand_aliasing={{0}: (6, {})} | custom-call | flops 899999989760 | tf_op jit(solution)/shard_map/attend/pallas_call | solution.py:44
  89.0 5.5 %collective-permute-done.11.refs_1_ = bf16[128,5120]{1,0:T(8,128)(2,1)} collective-permute-done((bf16[128,5120]{1,0:T(8,128)(2,1)}, bf16[128,5120]{1,0:T(8,128)(2,1)}, u32[]{:S(2)}, u32[]{:S(2)}) %collective-permute-start.11) | collective-permute-done | bytes 1310752 | tf_op jit(solution)/shard_map/ppermute | solution.py:547
  105.5 11.4 %attend.3 = (bf16[512,2048]{1,0:T(8,128)(2,1)}, f32[4,4,512]{2,1,0:T(4,128)}) custom-call(s32[4]{0:T(128)} %pad_add_fusion.refs_0_, bf16[512,1024]{1,0:T(8,128)(2,1)} %get-tuple-element.100.refs_1_, bf16[512,1024]{1,0:T(8,128)(2,1)} %get-tuple-element.101.refs_2_, ...), custom_call_target="tpu_custom_call", output_to_operand_aliasing={{0}: (6, {}), {1}: (7, {})} | custom-call | flops 899999989760 | tf_op jit(solution)/shard_map/attend/pallas_call | solution.py:44
  126.3 7.6 %output.1 = (bf16[1024,1024]{1,0:T(8,128)(2,1)}, f32[512,1024]{1,0:T(8,128)}, f32[512,1]{1,0:T(8,128)}, bf16[512,1024]{1,0:T(8,128)(2,1)}, bf16[512,1536]{1,0:T(8,128)(2,1)}) custom-call(s32[4]{0:T(128)} %pad_add_fusion.refs_0_, bf16[512,2048]{1,0:T(8,128)(2,1)} %get-tuple-element.106.refs_1_.refs_2_, bf16[512,2048]{1,0:T(8,128)(2,1)} %get-tuple-element.106.refs_1_.refs_2_, ...), custom_call_target="tpu_custom_call" | custom-call | flops 599999971328 | tf_op jit(solution)/shard_map/output/pallas_call | solution.py:44
  134.0 42.8 %feed_forward.1 = (bf16[512,4096]{1,0:T(8,128)(2,1)}, bf16[512,2048]{1,0:T(8,128)(2,1)}, bf16[256,1024]{1,0:T(8,128)(2,1)}, bf16[256,1024]{1,0:T(8,128)(2,1)}, b...) custom-call(s32[4]{0:T(128)} %pad_add_fusion.refs_0_, ...), custom_call_target="tpu_custom_call" | custom-call | flops 3999999983616 | tf_op jit(solution)/shard_map/feed_forward/pallas_call | solution.py:44
  177.9 10.1 %attend_back.2 = (bf16[512,1024]{1,0:T(8,128)(2,1)}, bf16[512,4096]{1,0:T(8,128)(2,1)}, f32[512,512]{1,0:T(8,128)}, bf16[512,512]{1,0:T(8,128)(2,1)}) custom-call(s32[4]{0:T(128)} %pad_add_fusion.refs_0_, bf16[512,1024]{1,0:T(8,128)(2,1)} %get-tuple-element.100.refs_1_, ...), custom_call_target="tpu_custom_call", output_to_operand_aliasing={{1}: (8, {})} | custom-call | flops 1500000026624 | tf_op jit(solution)/shard_map/attend_back/pallas_call | solution.py:44
  188.4 7.3 %grad_x.3.refs_5_ = bf16[1024,1024]{1,0:T(8,128)(2,1)} custom-call(s32[4]{0:T(128)} %pad_add_fusion.refs_0_, bf16[512,4096]{1,0:T(8,128)(2,1)} %get-tuple-element.123.refs_1_, bf16[512,1024]{1,0:T(8,128)(2,1)} %get-tuple-element.124.refs_2_, bf16[512,2048]{1,0:T(8,128)(2,1)} %collective-permute-done.18.refs_3_, ...), custom_call_target="tpu_custom_call" | custom-call | flops 799999983616 | tf_op jit(solution)/shard_map/grad_x/pallas_call | solution.py:44
  195.8 7.8 %grad_x.4.refs_10_ = bf16[1024,1024]{1,0:T(8,128)(2,1)} custom-call(s32[4]{0:T(128)} %pad_add_fusion.refs_0_, bf16[512,1024]{1,0:T(8,128)(2,1)} %get-tuple-element.109.refs_1_, bf16[512,4096]{1,0:T(8,128)(2,1)} %get-tuple-element.121.refs_2_, bf16[512,1536]{1,0:T(8,128)(2,1)} %collective-permute-done.16.refs_3_, ...), custom_call_target="tpu_custom_call" | custom-call | flops 799999983616 | tf_op jit(solution)/shard_map/grad_x/pallas_call | solution.py:44
  205.5 23.9 %attend_back.3 = (bf16[512,1024]{1,0:T(8,128)(2,1)}, bf16[512,4096]{1,0:T(8,128)(2,1)}, f32[512,1536]{1,0:T(8,128)}, bf16[512,1536]{1,0:T(8,128)(2,1)}) custom-call(s32[4]{0:T(128)} %pad_add_fusion.refs_0_, bf16[512,1024]{1,0:T(8,128)(2,1)} %get-tuple-element.100.refs_1_, ...), custom_call_target="tpu_custom_call", output_to_operand_aliasing={{1}: (8, {}), {0}: (9, {})} | custom-call | flops 1500000026624 | tf_op jit(solution)/shard_map/attend_back/pallas_call | solution.py:44
  229.9 5.3 %input_query.1.refs_11_.refs_3_ = f32[512,1024]{1,0:T(8,128)} custom-call(s32[4]{0:T(128)} %pad_add_fusion.refs_0_, bf16[512,1024]{1,0:T(8,128)(2,1)} %get-tuple-element.130.refs_1_.refs_9_, bf16[1024,3072]{1,0:T(8,128)(2,1)} %get-tuple-element.132.refs_2_, f32[512,1024]{1,0:T(8,128)} %get-tuple-element.133.refs_3_, ...), custom_call_target="tpu_custom_call" | custom-call | flops 499999997952 | tf_op jit(solution)/shard_map/input_query/pallas_call | solution.py:44
  235.2 6.7 %delta.1 = (bf16[512,1024]{1,0:T(8,128)(2,1)}, bf16[512,1024]{1,0:T(8,128)(2,1)}, bf16[512,4096]{1,0:T(8,128)(2,1)}, f32[8,1024]{1,0:T(8,128)}) custom-call(s32[4]{0:T(128)} %pad_add_fusion.refs_0_, f32[512,512]{1,0:T(8,128)} %get-tuple-element.118.refs_5_.refs_1_, ...), custom_call_target="tpu_custom_call", output_to_operand_aliasing={{2}: (10, {})} | custom-call | flops 499999997952 | tf_op jit(solution)/shard_map/delta/pallas_call | solution.py:44
  242.4 7.7 %input.1 = (f32[256,1024]{1,0:T(8,128)}, bf16[256,1024]{1,0:T(8,128)(2,1)}, f32[1,1024]{1,0:T(1,128)}) custom-call(s32[4]{0:T(128)} %pad_add_fusion.refs_0_, bf16[512,4096]{1,0:T(8,128)(2,1)} %get-tuple-element.134.refs_1_.refs_2_, bf16[1024,3072]{1,0:T(8,128)(2,1)} %get-tuple-element.132.refs_2_, f32[512,1024]{1,0:T(8,128)} %input_query.1.refs_11_.refs_3_, ...), custom_call_target="tpu_custom_call" | custom-call | flops 799999983616 | tf_op jit(solution)/shard_map/input/pallas_call | solution.py:44
  253.1 7.2 %grad_y.4 = (bf16[512,1024]{1,0:T(8,128)(2,1)}, bf16[512,1024]{1,0:T(8,128)(2,1)S(1)}) custom-call(s32[4]{0:T(128)S(1)} %copy-done.2, bf16[512,4096]{1,0:T(8,128)(2,1)S(1)} %copy-done.16, bf16[512,1024]{1,0:T(8,128)(2,1)S(1)} %copy-done.9, bf16[512,2048]{1,0:T(8,128)(2,1)} %collective-permute-done.18.refs_3_, ...), custom_call_target="tpu_custom_call" | custom-call | flops 499999997952 | tf_op jit(solution)/shard_map/grad_y/pallas_call | solution.py:44
  261.7 9.3 %grad_x.5.refs_6_ = bf16[1024,1024]{1,0:T(8,128)(2,1)} custom-call(s32[4]{0:T(128)} %pad_add_fusion.refs_0_, bf16[512,2048]{1,0:T(8,128)(2,1)} %get-tuple-element.106.refs_1_.refs_2_, bf16[512,4096]{1,0:T(8,128)(2,1)} %get-tuple-element.134.refs_1_.refs_2_, bf16[512,1536]{1,0:T(8,128)(2,1)} %collective-permute-done.16.refs_3_, ...), custom_call_target="tpu_custom_call" | custom-call | flops 799999983616 | tf_op jit(solution)/shard_map/grad_x/pallas_call | solution.py:44
  274.5 12.3 %collective-permute-done.28.refs_2_.refs_4_ = bf16[512,1024]{1,0:T(8,128)(2,1)} collective-permute-done((bf16[512,1024]{1,0:T(8,128)(2,1)}, bf16[512,1024]{1,0:T(8,128)(2,1)}, u32[]{:S(2)}, u32[]{:S(2)}) %collective-permute-start.28) | collective-permute-done | bytes 1048608 | tf_op jit(solution)/shard_map/ppermute | solution.py:547
  293.4 7.5 %grad_y.5 = (bf16[512,1024]{1,0:T(8,128)(2,1)}, bf16[512,1024]{1,0:T(8,128)(2,1)S(1)}) custom-call(s32[4]{0:T(128)S(1)} %copy-done.3, bf16[512,1024]{1,0:T(8,128)(2,1)S(1)} %copy-done.28, bf16[512,4096]{1,0:T(8,128)(2,1)S(1)} %copy-done.7, bf16[512,1536]{1,0:T(8,128)(2,1)} %collective-permute-done.16.refs_3_, ...), custom_call_target="tpu_custom_call" | custom-call | flops 499999997952 | tf_op jit(solution)/shard_map/grad_y/pallas_call | solution.py:44
  308.1 17.0 %collective-permute-done.33.refs_2_.refs_4_ = bf16[512,1024]{1,0:T(8,128)(2,1)} collective-permute-done((bf16[512,1024]{1,0:T(8,128)(2,1)}, bf16[512,1024]{1,0:T(8,128)(2,1)}, u32[]{:S(2)}, u32[]{:S(2)}) %collective-permute-start.33) | collective-permute-done | bytes 1048608 | tf_op jit(solution)/shard_map/ppermute | solution.py:547
  334.3 5.3 %grad_y.6 = (bf16[256,1024]{1,0:T(8,128)(2,1)}, bf16[256,1024]{1,0:T(8,128)(2,1)S(1)}) custom-call(s32[4]{0:T(128)S(1)} %copy-done.3, bf16[512,2048]{1,0:T(8,128)(2,1)S(1)} %copy-done.17, bf16[512,4096]{1,0:T(8,128)(2,1)S(1)} %copy-done.15, bf16[512,1536]{1,0:T(8,128)(2,1)} %collective-permute-done.16.refs_3_, ...), custom_call_target="tpu_custom_call" | custom-call | flops 499999997952 | tf_op jit(solution)/shard_map/grad_y/pallas_call | solution.py:44
  339.9 5.3 %grad_y.7 = (bf16[256,1024]{1,0:T(8,128)(2,1)}, bf16[256,1024]{1,0:T(8,128)(2,1)S(1)}) custom-call(s32[4]{0:T(128)S(1)} %copy-done.3, bf16[512,2048]{1,0:T(8,128)(2,1)S(1)} %copy-done.17, bf16[512,4096]{1,0:T(8,128)(2,1)S(1)} %copy-done.15, bf16[512,1536]{1,0:T(8,128)(2,1)} %collective-permute-done.16.refs_3_, ...), custom_call_target="tpu_custom_call" | custom-call | flops 499999997952 | tf_op jit(solution)/shard_map/grad_y/pallas_call | solution.py:44
  393.9 5.3 %grad_out.2.refs_3_ = f32[1024,1024]{1,0:T(8,128)} custom-call(s32[4]{0:T(128)} %pad_add_fusion.refs_0_, bf16[512,1024]{1,0:T(8,128)(2,1)} %grad_join.4.refs_3_.refs_1_, bf16[512,1024]{1,0:T(8,128)(2,1)} %collective-permute-done.46.refs_2_, f32[32,1024]{1,0:T(8,128)} %lines_add.7.refs_3_.refs_1_), custom_call_target="tpu_custom_call" | custom-call | flops 299999985664 | tf_op jit(solution)/shard_map/grad_out/pallas_call | solution.py:44
  433.9 5.2 %grad_out.3.refs_3_ = f32[256,4096]{1,0:T(8,128)} custom-call(s32[4]{0:T(128)} %pad_add_fusion.refs_0_, bf16[512,1024]{1,0:T(8,128)(2,1)} %grad_join.5.refs_3_.refs_1_, bf16[512,1024]{1,0:T(8,128)(2,1)} %collective-permute-done.49.refs_2_, f32[32,1024]{1,0:T(8,128)} %lines_add.8.refs_3_.refs_1_), custom_call_target="tpu_custom_call" | custom-call | flops 299999985664 | tf_op jit(solution)/shard_map/grad_out/pallas_call | solution.py:44
  (243 shorter events, 207.0 us)
Async XLA Ops:
  7.2 126.8 %all-gather.2.cloned.1.call-start = ((), (), s32[]{:S(2)}) async-start(), calls=%async_computation | async-start | bytes 10485760 | tf_op jit(solution)/shard_map/all_gather | solution.py:603
  16.2 27.9 %collective-permute-start = (bf16[128,3072]{1,0:T(8,128)(2,1)}, bf16[128,3072]{1,0:T(8,128)(2,1)}, u32[]{:S(2)}, u32[]{:S(2)}) collective-permute-start(bf16[128,3072]{1,0:T(8,128)(2,1)} %cut.2.refs_4_), channel_id=1, source_target_pairs={{0,2},{1,3},{2,0},{3,1},{4,6},{5,7},{6,4},{7,5},{8,10},{9,11},{10,... | collective-permute-start | bytes 2359304 | tf_op jit(solution)/shard_map/ppermute | solution.py:547
  19.5 24.6 %collective-permute-start.1 = (bf16[256,3072]{1,0:T(8,128)(2,1)}, bf16[256,3072]{1,0:T(8,128)(2,1)}, u32[]{:S(2)}, u32[]{:S(2)}) collective-permute-start(bf16[256,3072]{1,0:T(8,128)(2,1)} %pack.2.refs_3_.refs_4_), channel_id=1, source_target_pairs={{0,1},{1,0},{2,3},{3,2},{4,5},{5,4},{6,7},{7,6},{8,9},{9,8},{10,11... | collective-permute-start | bytes 4718600 | tf_op jit(solution)/shard_map/ppermute | solution.py:547
  32.1 62.4 %collective-permute-start.11 = (bf16[128,5120]{1,0:T(8,128)(2,1)}, bf16[128,5120]{1,0:T(8,128)(2,1)}, u32[]{:S(2)}, u32[]{:S(2)}) collective-permute-start(bf16[128,5120]{1,0:T(8,128)(2,1)} %cut.3.refs_2_), channel_id=1, source_target_pairs={{0,2},{1,3},{2,0},{3,1},{4,6},{5,7},{6,4},{7,5},{8,10},{9,11},{10,... | collective-permute-start | bytes 3932168 | tf_op jit(solution)/shard_map/ppermute | solution.py:547
  103.1 30.9 %collective-permute-start.15 = (bf16[256,1024]{1,0:T(8,128)(2,1)}, bf16[256,1024]{1,0:T(8,128)(2,1)}, u32[]{:S(2)}, u32[]{:S(2)}) collective-permute-start(bf16[256,1024]{1,0:T(8,128)(2,1)} %pick.6.refs_8_), channel_id=1, source_target_pairs={{0,2},{1,3},{2,0},{3,1},{4,6},{5,7},{6,4},{7,5},{8,10},{9,11},{10,... | collective-permute-start | bytes 1572872 | tf_op jit(solution)/shard_map/ppermute | solution.py:547
  133.9 61.9 %collective-permute-start.16 = (bf16[512,1536]{1,0:T(8,128)(2,1)}, bf16[512,1536]{1,0:T(8,128)(2,1)}, u32[]{:S(2)}, u32[]{:S(2)}) collective-permute-start(bf16[512,1536]{1,0:T(8,128)(2,1)} %get-tuple-element.122), channel_id=1, source_target_pairs={{0,1},{1,0},{2,3},{3,2},{4,5},{5,4},{6,7},{7,6},{8,9},{9,8},{10,11... | collective-permute-start | bytes 4718600 | tf_op jit(solution)/shard_map/ppermute | solution.py:547
  195.7 54.5 %collective-permute-start.26 = (bf16[1024,1024]{1,0:T(8,128)(2,1)}, bf16[1024,1024]{1,0:T(8,128)(2,1)}, u32[]{:S(2)}, u32[]{:S(2)}) collective-permute-start(bf16[1024,1024]{1,0:T(8,128)(2,1)} %grad_x.3.refs_5_), channel_id=1, source_target_pairs={{0,2},{1,3},{2,0},{3,1},{4,6},{5,7},{6,4},{7,5},{8,10},{9,11},{10,... | collective-permute-start | bytes 6291464 | tf_op jit(solution)/shard_map/ppermute | solution.py:547
  203.7 89.8 %collective-permute-start.30 = (bf16[1024,1024]{1,0:T(8,128)(2,1)}, bf16[1024,1024]{1,0:T(8,128)(2,1)}, u32[]{:S(2)}, u32[]{:S(2)}) collective-permute-start(bf16[1024,1024]{1,0:T(8,128)(2,1)} %grad_x.4.refs_10_), channel_id=1, source_target_pairs={{0,2},{1,3},{2,0},{3,1},{4,6},{5,7},{6,4},{7,5},{8,10},{9,11},{10,... | collective-permute-start | bytes 6291464 | tf_op jit(solution)/shard_map/ppermute | solution.py:547
  229.4 32.1 %collective-permute-start.23 = (bf16[512,1024]{1,0:T(8,128)(2,1)}, bf16[512,1024]{1,0:T(8,128)(2,1)}, u32[]{:S(2)}, u32[]{:S(2)}) collective-permute-start(bf16[512,1024]{1,0:T(8,128)(2,1)} %get-tuple-element.130.refs_1_.refs_9_), channel_id=1, source_target_pairs={{0,1},{1,0},{2,3},{3,2},{4,5},{5,4},{6,7},{7,6},{8,9},{9,8},{10,11... | collective-permute-start | bytes 3145736 | tf_op jit(solution)/shard_map/ppermute | solution.py:547
  261.3 25.5 %collective-permute-start.28 = (bf16[512,1024]{1,0:T(8,128)(2,1)}, bf16[512,1024]{1,0:T(8,128)(2,1)}, u32[]{:S(2)}, u32[]{:S(2)}) collective-permute-start(bf16[512,1024]{1,0:T(8,128)(2,1)} %get-tuple-element.140), channel_id=1, source_target_pairs={{0,4},{4,0},{8,12},{12,8},{16,20},{20,16},{24,28},{28,24},{1,5},{5... | collective-permute-start | bytes 3145736 | tf_op jit(solution)/shard_map/ppermute | solution.py:547
  271.0 63.4 %collective-permute-start.27 = (bf16[1024,1024]{1,0:T(8,128)(2,1)}, bf16[1024,1024]{1,0:T(8,128)(2,1)}, u32[]{:S(2)}, u32[]{:S(2)}) collective-permute-start(bf16[1024,1024]{1,0:T(8,128)(2,1)} %grad_x.5.refs_6_), channel_id=1, source_target_pairs={{0,2},{1,3},{2,0},{3,1},{4,6},{5,7},{6,4},{7,5},{8,10},{9,11},{10,... | collective-permute-start | bytes 6291464 | tf_op jit(solution)/shard_map/ppermute | solution.py:547
  292.3 65.1 %collective-permute-start.36 = (f32[32,1024]{1,0:T(8,128)}, f32[32,1024]{1,0:T(8,128)}, u32[]{:S(2)}, u32[]{:S(2)}) collective-permute-start(f32[32,1024]{1,0:T(8,128)} %lines_add.5.refs_6_.refs_1_), channel_id=1, source_target_pairs={{0,2},{1,3},{2,0},{3,1},{4,6},{5,7},{6,4},{7,5},{8,10},{9,11},{10,... | collective-permute-start | bytes 393224 | tf_op jit(solution)/shard_map/ppermute | solution.py:547
  301.0 24.1 %collective-permute-start.33 = (bf16[512,1024]{1,0:T(8,128)(2,1)}, bf16[512,1024]{1,0:T(8,128)(2,1)}, u32[]{:S(2)}, u32[]{:S(2)}) collective-permute-start(bf16[512,1024]{1,0:T(8,128)(2,1)} %get-tuple-element.147), channel_id=1, source_target_pairs={{0,4},{4,0},{8,12},{12,8},{16,20},{20,16},{24,28},{28,24},{1,5},{5... | collective-permute-start | bytes 3145736 | tf_op jit(solution)/shard_map/ppermute | solution.py:547
  305.3 24.6 %collective-permute-start.32 = (bf16[256,1024]{1,0:T(8,128)(2,1)}, bf16[256,1024]{1,0:T(8,128)(2,1)}, u32[]{:S(2)}, u32[]{:S(2)}) collective-permute-start(bf16[256,1024]{1,0:T(8,128)(2,1)} %grad_add.8.refs_5_.refs_1_), channel_id=1, source_target_pairs={{0,16},{4,20},{8,24},{12,28},{16,0},{20,4},{24,8},{28,12},{1,17},{... | collective-permute-start | bytes 1572872 | tf_op jit(solution)/shard_map/ppermute | solution.py:547
  339.7 22.6 %collective-permute-start.35 = (bf16[256,1024]{1,0:T(8,128)(2,1)}, bf16[256,1024]{1,0:T(8,128)(2,1)}, u32[]{:S(2)}, u32[]{:S(2)}) collective-permute-start(bf16[256,1024]{1,0:T(8,128)(2,1)} %get-tuple-element.152), channel_id=1, source_target_pairs={{0,4},{4,0},{8,12},{12,8},{16,20},{20,16},{24,28},{28,24},{1,5},{5... | collective-permute-start | bytes 1572872 | tf_op jit(solution)/shard_map/ppermute | solution.py:547
  349.5 24.6 %collective-permute-start.42 = (bf16[256,1024]{1,0:T(8,128)(2,1)}, bf16[256,1024]{1,0:T(8,128)(2,1)}, u32[]{:S(2)}, u32[]{:S(2)}) collective-permute-start(bf16[256,1024]{1,0:T(8,128)(2,1)} %grad_add.10.refs_3_.refs_1_), channel_id=1, source_target_pairs={{0,16},{4,20},{8,24},{12,28},{16,0},{20,4},{24,8},{28,12},{1,17},{... | collective-permute-start | bytes 1572872 | tf_op jit(solution)/shard_map/ppermute | solution.py:547
  356.7 37.0 %collective-permute-start.46 = (bf16[512,1024]{1,0:T(8,128)(2,1)}, bf16[512,1024]{1,0:T(8,128)(2,1)}, u32[]{:S(2)}, u32[]{:S(2)}) collective-permute-start(bf16[512,1024]{1,0:T(8,128)(2,1)} %grad_join.4.refs_3_.refs_1_), channel_id=1, source_target_pairs={{0,4},{4,0},{8,12},{12,8},{16,20},{20,16},{24,28},{28,24},{1,5},{5... | collective-permute-start | bytes 3145736 | tf_op jit(solution)/shard_map/ppermute | solution.py:547
  359.6 29.5 %collective-permute-start.47 = (f32[32,1024]{1,0:T(8,128)}, f32[32,1024]{1,0:T(8,128)}, u32[]{:S(2)}, u32[]{:S(2)}) collective-permute-start(f32[32,1024]{1,0:T(8,128)} %lines_add.6.refs_5_.refs_1_), channel_id=1, source_target_pairs={{0,4},{4,0},{8,12},{12,8},{16,20},{20,16},{24,28},{28,24},{1,5},{5... | collective-permute-start | bytes 393224 | tf_op jit(solution)/shard_map/ppermute | solution.py:547
  374.1 43.3 %collective-permute-start.39 = (bf16[256,1024]{1,0:T(8,128)(2,1)}, bf16[256,1024]{1,0:T(8,128)(2,1)}, u32[]{:S(2)}, u32[]{:S(2)}) collective-permute-start(bf16[256,1024]{1,0:T(8,128)(2,1)} %relay.2.refs_3_), channel_id=1, source_target_pairs={{0,2},{1,3},{2,0},{3,1},{4,6},{5,7},{6,4},{7,5},{8,10},{9,11},{10,... | collective-permute-start | bytes 1572872 | tf_op jit(solution)/shard_map/ppermute | solution.py:547
  379.8 22.8 %collective-permute-start.45 = (bf16[256,1024]{1,0:T(8,128)(2,1)}, bf16[256,1024]{1,0:T(8,128)(2,1)}, u32[]{:S(2)}, u32[]{:S(2)}) collective-permute-start(bf16[256,1024]{1,0:T(8,128)(2,1)} %grad_add.11.refs_3_.refs_1_), channel_id=1, source_target_pairs={{0,8},{4,12},{8,0},{12,4},{16,24},{20,28},{24,16},{28,20},{1,9},{5... | collective-permute-start | bytes 1572872 | tf_op jit(solution)/shard_map/ppermute | solution.py:547
  385.4 23.9 %collective-permute-start.44 = (bf16[128,1024]{1,0:T(8,128)(2,1)}, bf16[128,1024]{1,0:T(8,128)(2,1)}, u32[]{:S(2)}, u32[]{:S(2)}) collective-permute-start(bf16[128,1024]{1,0:T(8,128)(2,1)} %grad_add.12.refs_3_.refs_1_), channel_id=1, source_target_pairs={{0,16},{4,20},{8,24},{12,28},{16,0},{20,4},{24,8},{28,12},{1,17},{... | collective-permute-start | bytes 786440 | tf_op jit(solution)/shard_map/ppermute | solution.py:547
  393.7 35.1 %collective-permute-start.50 = (f32[32,1024]{1,0:T(8,128)}, f32[32,1024]{1,0:T(8,128)}, u32[]{:S(2)}, u32[]{:S(2)}) collective-permute-start(f32[32,1024]{1,0:T(8,128)} %lines_add.7.refs_3_.refs_1_), channel_id=1, source_target_pairs={{0,8},{4,12},{8,0},{12,4},{16,24},{20,28},{24,16},{28,20},{1,9},{5... | collective-permute-start | bytes 393224 | tf_op jit(solution)/shard_map/ppermute | solution.py:547
  407.5 26.4 %collective-permute-start.49 = (bf16[512,1024]{1,0:T(8,128)(2,1)}, bf16[512,1024]{1,0:T(8,128)(2,1)}, u32[]{:S(2)}, u32[]{:S(2)}) collective-permute-start(bf16[512,1024]{1,0:T(8,128)(2,1)} %grad_join.5.refs_3_.refs_1_), channel_id=1, source_target_pairs={{0,4},{4,0},{8,12},{12,8},{16,20},{20,16},{24,28},{28,24},{1,5},{5... | collective-permute-start | bytes 3145736 | tf_op jit(solution)/shard_map/ppermute | solution.py:547
  428.3 25.5 %collective-permute-start.55 = (bf16[256,1024]{1,0:T(8,128)(2,1)}, bf16[256,1024]{1,0:T(8,128)(2,1)}, u32[]{:S(2)}, u32[]{:S(2)}) collective-permute-start(bf16[256,1024]{1,0:T(8,128)(2,1)} %grad_join.7.refs_3_.refs_1_), channel_id=1, source_target_pairs={{0,4},{4,0},{8,12},{12,8},{16,20},{20,16},{24,28},{28,24},{1,5},{5... | collective-permute-start | bytes 1572872 | tf_op jit(solution)/shard_map/ppermute | solution.py:547
  (72 other events, 681.6 us)
Sparse Core Ops, SparseCore 0:
  38.0 90.8 all-gather.1

commit v3 on v2

--- a/solution.py
+++ b/solution.py
@@ -594,15 +594,17 @@
     two_sibling = swap_core(two_own)
     two_cut = cut(two_weights, tokens_got, two_own)
     two_first = swap_chip(two_cut)
-    down_copy = run("copy", copy_kernel, (1,), [whole(down_weight)], [whole_out(down_weight.shape, BF16)], (two_cut,))
+    upstream_away = pick(upstream, 1, two_cut)
+    upstream_got = swap_chip(upstream_away)
+    tokens_mine = pick(inputs, 0, upstream_away)
     live = chip < bucket_count[bucket]
     seq_weight = live.astype(F32) * (2 * n_dp / jnp.sum(bucket_count).astype(F32))
     small_two = jnp.concatenate([small, tokens_got[half:]], axis=0)
     small_far = swap_core(small_two)
-    three_parts, split_done = split(three_first, three_sibling, two_sibling, down_copy, small_far)
+    three_parts, split_done = split(three_first, three_sibling, two_sibling, tokens_mine, small_far)
+    down_copy = run("copy", copy_kernel, (1,), [whole(down_weight)], [whole_out(down_weight.shape, BF16)], (split_done,))
     down_matrix = lax.all_gather(down_copy, "fsdp", axis=0, tiled=True)
-    tokens_mine = pick(inputs, 0, split_done)
-    query_remote, kv_remote = remote(three_parts, (D, 2 * D), tokens_mine)
+    query_remote, kv_remote = remote(three_parts, (D, 2 * D), down_copy)
     lines, up_bias = run(
         "lines_in", lines_in_kernel, (1,),
         [whole(a) for a in (small_two, small_far, sinusoid(timestep), seq_weight.reshape(1, 1))],
@@ -645,9 +647,7 @@
 
     lefts, lse = attend(0, groups // 2, lefts, None)
     two_parts, split_done = split(two_first, lse)
-    upstream_away = pick(upstream, 1, split_done)
-    upstream_got = swap_chip(upstream_away)
-    lefts, lse = attend(groups // 2, groups // 2, lefts, lse, upstream_away)
+    lefts, lse = attend(groups // 2, groups // 2, lefts, lse, split_done)
     two_remote = remote(two_parts, (two_own.shape[1],), lse)
     upstream_mine = pick(upstream, 0, two_remote)
     two_pieces = [two_own, two_remote, two_sibling, swap_core(two_remote)]

time: 469 us -> 466 us (level)
  waiting for transfers between devices: 74 us -> 64.5 us
  starting transfers between devices: 45.4 us -> 51.4 us
    ppermute x56, waiting for transfers between devices: 74 us -> 60.9 us  [swap(): return lax.ppermute(value, axis, [(i, i ^ bit) for i in range(size)])]
    ppermute x56, starting transfers between devices: 45.3 us -> 51.3 us  [swap(): return lax.ppermute(value, axis, [(i, i ^ bit) for i in range(size)])]
where the time goes in v3:
time: 466 us; the launch traced here: 461 us
  Pallas kernels  311 us (67%)
  waiting for transfers between devices  64.5 us (14%)
  starting transfers between devices  51.4 us (11%)
  between operations  16.1 us (3%)
  local copies, waits for them, and re-layouts  15.2 us (3%)
    pallas_call x62, Pallas kernels, run_kernel(): pl.pallas_call(kernel, grid_spec=pltpu.PrefetchScalarGridSpec(num_scalar_...  311 us
    ppermute x56, waiting for transfers between devices, swap(): return lax.ppermute(value, axis, [(i, i ^ bit) for i in range(size)])  60.9 us
    ppermute x56, starting transfers between devices, swap(): return lax.ppermute(value, axis, [(i, i ^ bit) for i in range(size)])  51.3 us
    unnamed x76, local copies, waits for them, and re-layouts  11.2 us
  transfers between devices with their start and end apart: 57, of which 20 were waited for; matrix products, arithmetic and copies ran while one was open for 1% of the time, Pallas kernels for 66%

profile of v3, /device:TPU:0, one launch (start us, length us, event | category | flops | bytes accessed | tf_op | source)
XLA Modules:
  0.0 460.6 jit_solution(18234369979729247509)
XLA Ops:
  19.5 4.2 pack.3.refs_4_.refs_6_.refs_10_
  39.4 4.8 %collective-permute-done.2.refs_1_ = bf16[128,3072]{1,0:T(8,128)(2,1)} collective-permute-done((bf16[128,3072]{1,0:T(8,128)(2,1)}, bf16[128,3072]{1,0:T(8,128)(2,1)}, u32[]{:S(2)}, u32[]{:S(2)}) %collective-permute-start.2) | collective-permute-done | bytes 786464 | tf_op jit(solution)/shard_map/ppermute | solution.py:547
  64.2 8.9 %key_value.1 = (bf16[512,1024]{1,0:T(8,128)(2,1)}, bf16[512,1024]{1,0:T(8,128)(2,1)}, bf16[1024,3072]{1,0:T(8,128)(2,1)}, bf16[512,2048]{1,0:T(8,128)(2,1)}) custom-call(s32[4]{0:T(128)} %pad_add_fusion.refs_0_, bf16[256,1024]{1,0:T(8,128)(2,1)} %pick.6.refs_4_.refs_1_.refs_3_, bf16[272,1024]{1,0:T(8,128)(2,1)} %collective-permute-done.refs_3_.refs_2_.refs_4_, ...), custom_call_target="tpu_custom_call" | custom-call | flops 699999977472 | tf_op jit(solution)/shard_map/key_value/pallas_call | solution.py:44
  73.7 4.9 %query.1 = (bf16[512,1024]{1,0:T(8,128)(2,1)}, bf16[1024,3072]{1,0:T(8,128)(2,1)}) custom-call(s32[4]{0:T(128)} %pad_add_fusion.refs_0_, bf16[512,2048]{1,0:T(8,128)(2,1)} %get-tuple-element.97.refs_1_.refs_6_, f32[16,1024]{1,0:T(8,128)} %get-tuple-element.96.refs_3_.refs_2_.refs_5_.refs_7_, ...), custom_call_target="tpu_custom_call", output_to_operand_aliasing={{1}: (7, {})} | custom-call | flops 399999991808 | tf_op jit(solution)/shard_map/query/pallas_call | solution.py:44
  78.6 10.8 %attend.2 = (bf16[512,2048]{1,0:T(8,128)(2,1)}, f32[4,4,512]{2,1,0:T(4,128)}) custom-call(s32[4]{0:T(128)} %pad_add_fusion.refs_0_, bf16[512,1024]{1,0:T(8,128)(2,1)} %get-tuple-element.100.refs_1_, bf16[512,1024]{1,0:T(8,128)(2,1)} %get-tuple-element.101.refs_2_, bf16[512,1024]{1,0:T(8,128)(2,1)} %get-tuple-element.102.refs_3_, ...), custom_call_target="tpu_custom_call", output_to_operand_aliasing={{0}: (6, {})} | custom-call | flops 899999989760 | tf_op jit(solution)/shard_map/attend/pallas_call | solution.py:44
  95.1 11.3 %attend.3 = (bf16[512,2048]{1,0:T(8,128)(2,1)}, f32[4,4,512]{2,1,0:T(4,128)}) custom-call(s32[4]{0:T(128)} %pad_add_fusion.refs_0_, bf16[512,1024]{1,0:T(8,128)(2,1)} %get-tuple-element.100.refs_1_, bf16[512,1024]{1,0:T(8,128)(2,1)} %get-tuple-element.101.refs_2_, ...), custom_call_target="tpu_custom_call", output_to_operand_aliasing={{0}: (6, {}), {1}: (7, {})} | custom-call | flops 899999989760 | tf_op jit(solution)/shard_map/attend/pallas_call | solution.py:44
  119.8 7.5 %output.1 = (bf16[1024,1024]{1,0:T(8,128)(2,1)}, f32[512,1024]{1,0:T(8,128)}, f32[512,1]{1,0:T(8,128)}, bf16[512,1024]{1,0:T(8,128)(2,1)}, bf16[512,1536]{1,0:T(8,128)(2,1)}) custom-call(s32[4]{0:T(128)} %pad_add_fusion.refs_0_, bf16[512,2048]{1,0:T(8,128)(2,1)} %get-tuple-element.106.refs_1_.refs_2_, bf16[512,2048]{1,0:T(8,128)(2,1)} %get-tuple-element.106.refs_1_.refs_2_, ...), custom_call_target="tpu_custom_call" | custom-call | flops 599999971328 | tf_op jit(solution)/shard_map/output/pallas_call | solution.py:44
  131.1 42.8 %feed_forward.1 = (bf16[512,4096]{1,0:T(8,128)(2,1)}, bf16[512,2048]{1,0:T(8,128)(2,1)}, bf16[256,1024]{1,0:T(8,128)(2,1)}, bf16[256,1024]{1,0:T(8,128)(2,1)}, b...) custom-call(s32[4]{0:T(128)} %pad_add_fusion.refs_0_, ...), custom_call_target="tpu_custom_call" | custom-call | flops 3999999983616 | tf_op jit(solution)/shard_map/feed_forward/pallas_call | solution.py:44
  175.0 10.1 %attend_back.2 = (bf16[512,1024]{1,0:T(8,128)(2,1)}, bf16[512,4096]{1,0:T(8,128)(2,1)}, f32[512,512]{1,0:T(8,128)}, bf16[512,512]{1,0:T(8,128)(2,1)}) custom-call(s32[4]{0:T(128)} %pad_add_fusion.refs_0_, bf16[512,1024]{1,0:T(8,128)(2,1)} %get-tuple-element.100.refs_1_, ...), custom_call_target="tpu_custom_call", output_to_operand_aliasing={{1}: (8, {})} | custom-call | flops 1500000026624 | tf_op jit(solution)/shard_map/attend_back/pallas_call | solution.py:44
  185.4 7.3 %grad_x.3.refs_5_ = bf16[1024,1024]{1,0:T(8,128)(2,1)} custom-call(s32[4]{0:T(128)} %pad_add_fusion.refs_0_, bf16[512,4096]{1,0:T(8,128)(2,1)} %get-tuple-element.123.refs_1_, bf16[512,1024]{1,0:T(8,128)(2,1)} %get-tuple-element.124.refs_2_, bf16[512,2048]{1,0:T(8,128)(2,1)} %collective-permute-done.18.refs_3_, ...), custom_call_target="tpu_custom_call" | custom-call | flops 799999983616 | tf_op jit(solution)/shard_map/grad_x/pallas_call | solution.py:44
  194.3 7.8 %grad_x.4.refs_10_ = bf16[1024,1024]{1,0:T(8,128)(2,1)} custom-call(s32[4]{0:T(128)} %pad_add_fusion.refs_0_, bf16[512,1024]{1,0:T(8,128)(2,1)} %get-tuple-element.109.refs_1_, bf16[512,4096]{1,0:T(8,128)(2,1)} %get-tuple-element.121.refs_2_, bf16[512,1536]{1,0:T(8,128)(2,1)} %collective-permute-done.16.refs_3_, ...), custom_call_target="tpu_custom_call" | custom-call | flops 799999983616 | tf_op jit(solution)/shard_map/grad_x/pallas_call | solution.py:44
  202.5 23.9 %attend_back.3 = (bf16[512,1024]{1,0:T(8,128)(2,1)}, bf16[512,4096]{1,0:T(8,128)(2,1)}, f32[512,1536]{1,0:T(8,128)}, bf16[512,1536]{1,0:T(8,128)(2,1)}) custom-call(s32[4]{0:T(128)} %pad_add_fusion.refs_0_, bf16[512,1024]{1,0:T(8,128)(2,1)} %get-tuple-element.100.refs_1_, ...), custom_call_target="tpu_custom_call", output_to_operand_aliasing={{1}: (8, {}), {0}: (9, {})} | custom-call | flops 1500000026624 | tf_op jit(solution)/shard_map/attend_back/pallas_call | solution.py:44
  226.9 5.3 %input_query.1.refs_11_.refs_3_ = f32[512,1024]{1,0:T(8,128)} custom-call(s32[4]{0:T(128)} %pad_add_fusion.refs_0_, bf16[512,1024]{1,0:T(8,128)(2,1)} %get-tuple-element.130.refs_1_.refs_9_, bf16[1024,3072]{1,0:T(8,128)(2,1)} %get-tuple-element.132.refs_2_, f32[512,1024]{1,0:T(8,128)} %get-tuple-element.133.refs_3_, ...), custom_call_target="tpu_custom_call" | custom-call | flops 499999997952 | tf_op jit(solution)/shard_map/input_query/pallas_call | solution.py:44
  232.2 6.7 %delta.1 = (bf16[512,1024]{1,0:T(8,128)(2,1)}, bf16[512,1024]{1,0:T(8,128)(2,1)}, bf16[512,4096]{1,0:T(8,128)(2,1)}, f32[8,1024]{1,0:T(8,128)}) custom-call(s32[4]{0:T(128)} %pad_add_fusion.refs_0_, f32[512,512]{1,0:T(8,128)} %get-tuple-element.118.refs_5_.refs_1_, ...), custom_call_target="tpu_custom_call", output_to_operand_aliasing={{2}: (10, {})} | custom-call | flops 499999997952 | tf_op jit(solution)/shard_map/delta/pallas_call | solution.py:44
  239.4 7.7 %input.1 = (f32[256,1024]{1,0:T(8,128)}, bf16[256,1024]{1,0:T(8,128)(2,1)}, f32[1,1024]{1,0:T(1,128)}) custom-call(s32[4]{0:T(128)} %pad_add_fusion.refs_0_, bf16[512,4096]{1,0:T(8,128)(2,1)} %get-tuple-element.134.refs_1_.refs_2_, bf16[1024,3072]{1,0:T(8,128)(2,1)} %get-tuple-element.132.refs_2_, f32[512,1024]{1,0:T(8,128)} %input_query.1.refs_11_.refs_3_, ...), custom_call_target="tpu_custom_call" | custom-call | flops 799999983616 | tf_op jit(solution)/shard_map/input/pallas_call | solution.py:44
  250.1 7.2 %grad_y.4 = (bf16[512,1024]{1,0:T(8,128)(2,1)}, bf16[512,1024]{1,0:T(8,128)(2,1)S(1)}) custom-call(s32[4]{0:T(128)S(1)} %copy-done.2, bf16[512,4096]{1,0:T(8,128)(2,1)S(1)} %copy-done.16, bf16[512,1024]{1,0:T(8,128)(2,1)S(1)} %copy-done.9, bf16[512,2048]{1,0:T(8,128)(2,1)} %collective-permute-done.18.refs_3_, ...), custom_call_target="tpu_custom_call" | custom-call | flops 499999997952 | tf_op jit(solution)/shard_map/grad_y/pallas_call | solution.py:44
  259.4 9.3 %grad_x.5.refs_6_ = bf16[1024,1024]{1,0:T(8,128)(2,1)} custom-call(s32[4]{0:T(128)} %pad_add_fusion.refs_0_, bf16[512,2048]{1,0:T(8,128)(2,1)} %get-tuple-element.106.refs_1_.refs_2_, bf16[512,4096]{1,0:T(8,128)(2,1)} %get-tuple-element.134.refs_1_.refs_2_, bf16[512,1536]{1,0:T(8,128)(2,1)} %collective-permute-done.16.refs_3_, ...), custom_call_target="tpu_custom_call" | custom-call | flops 799999983616 | tf_op jit(solution)/shard_map/grad_x/pallas_call | solution.py:44
  272.9 10.8 %collective-permute-done.28.refs_2_.refs_4_ = bf16[512,1024]{1,0:T(8,128)(2,1)} collective-permute-done((bf16[512,1024]{1,0:T(8,128)(2,1)}, bf16[512,1024]{1,0:T(8,128)(2,1)}, u32[]{:S(2)}, u32[]{:S(2)}) %collective-permute-start.28) | collective-permute-done | bytes 1048608 | tf_op jit(solution)/shard_map/ppermute | solution.py:547
  291.8 7.5 %grad_y.5 = (bf16[512,1024]{1,0:T(8,128)(2,1)}, bf16[512,1024]{1,0:T(8,128)(2,1)S(1)}) custom-call(s32[4]{0:T(128)S(1)} %copy-done.3, bf16[512,1024]{1,0:T(8,128)(2,1)S(1)} %copy-done.28, bf16[512,4096]{1,0:T(8,128)(2,1)S(1)} %copy-done.7, bf16[512,1536]{1,0:T(8,128)(2,1)} %collective-permute-done.16.refs_3_, ...), custom_call_target="tpu_custom_call" | custom-call | flops 499999997952 | tf_op jit(solution)/shard_map/grad_y/pallas_call | solution.py:44
  305.3 18.1 %collective-permute-done.33.refs_2_.refs_4_ = bf16[512,1024]{1,0:T(8,128)(2,1)} collective-permute-done((bf16[512,1024]{1,0:T(8,128)(2,1)}, bf16[512,1024]{1,0:T(8,128)(2,1)}, u32[]{:S(2)}, u32[]{:S(2)}) %collective-permute-start.33) | collective-permute-done | bytes 1048608 | tf_op jit(solution)/shard_map/ppermute | solution.py:547
  331.3 5.3 %grad_y.6 = (bf16[256,1024]{1,0:T(8,128)(2,1)}, bf16[256,1024]{1,0:T(8,128)(2,1)S(1)}) custom-call(s32[4]{0:T(128)S(1)} %copy-done.3, bf16[512,2048]{1,0:T(8,128)(2,1)S(1)} %copy-done.17, bf16[512,4096]{1,0:T(8,128)(2,1)S(1)} %copy-done.15, bf16[512,1536]{1,0:T(8,128)(2,1)} %collective-permute-done.16.refs_3_, ...), custom_call_target="tpu_custom_call" | custom-call | flops 499999997952 | tf_op jit(solution)/shard_map/grad_y/pallas_call | solution.py:44
  337.6 5.3 %grad_y.7 = (bf16[256,1024]{1,0:T(8,128)(2,1)}, bf16[256,1024]{1,0:T(8,128)(2,1)S(1)}) custom-call(s32[4]{0:T(128)S(1)} %copy-done.3, bf16[512,2048]{1,0:T(8,128)(2,1)S(1)} %copy-done.17, bf16[512,4096]{1,0:T(8,128)(2,1)S(1)} %copy-done.15, bf16[512,1536]{1,0:T(8,128)(2,1)} %collective-permute-done.16.refs_3_, ...), custom_call_target="tpu_custom_call" | custom-call | flops 499999997952 | tf_op jit(solution)/shard_map/grad_y/pallas_call | solution.py:44
  392.3 5.3 %grad_out.2.refs_3_ = f32[1024,1024]{1,0:T(8,128)} custom-call(s32[4]{0:T(128)} %pad_add_fusion.refs_0_, bf16[512,1024]{1,0:T(8,128)(2,1)} %grad_join.4.refs_3_.refs_1_, bf16[512,1024]{1,0:T(8,128)(2,1)} %collective-permute-done.46.refs_2_, f32[32,1024]{1,0:T(8,128)} %lines_add.7.refs_3_.refs_1_), custom_call_target="tpu_custom_call" | custom-call | flops 299999985664 | tf_op jit(solution)/shard_map/grad_out/pallas_call | solution.py:44
  431.7 5.2 %grad_out.3.refs_3_ = f32[256,4096]{1,0:T(8,128)} custom-call(s32[4]{0:T(128)} %pad_add_fusion.refs_0_, bf16[512,1024]{1,0:T(8,128)(2,1)} %grad_join.5.refs_3_.refs_1_, bf16[512,1024]{1,0:T(8,128)(2,1)} %collective-permute-done.49.refs_2_, f32[32,1024]{1,0:T(8,128)} %lines_add.8.refs_3_.refs_1_), custom_call_target="tpu_custom_call" | custom-call | flops 299999985664 | tf_op jit(solution)/shard_map/grad_out/pallas_call | solution.py:44
  (243 shorter events, 206.4 us)
Async XLA Ops:
  7.2 123.9 %all-gather.2.cloned.1.call-start = ((), (), s32[]{:S(2)}) async-start(), calls=%async_computation | async-start | bytes 10485760 | tf_op jit(solution)/shard_map/all_gather | solution.py:606
  16.2 27.9 %collective-permute-start.2 = (bf16[128,3072]{1,0:T(8,128)(2,1)}, bf16[128,3072]{1,0:T(8,128)(2,1)}, u32[]{:S(2)}, u32[]{:S(2)}) collective-permute-start(bf16[128,3072]{1,0:T(8,128)(2,1)} %cut.2.refs_4_), channel_id=1, source_target_pairs={{0,2},{1,3},{2,0},{3,1},{4,6},{5,7},{6,4},{7,5},{8,10},{9,11},{10,... | collective-permute-start | bytes 2359304 | tf_op jit(solution)/shard_map/ppermute | solution.py:547
  19.5 24.6 %collective-permute-start.3 = (bf16[256,3072]{1,0:T(8,128)(2,1)}, bf16[256,3072]{1,0:T(8,128)(2,1)}, u32[]{:S(2)}, u32[]{:S(2)}) collective-permute-start(bf16[256,3072]{1,0:T(8,128)(2,1)} %pack.2.refs_3_.refs_4_), channel_id=1, source_target_pairs={{0,1},{1,0},{2,3},{3,2},{4,5},{5,4},{6,7},{7,6},{8,9},{9,8},{10,11... | collective-permute-start | bytes 4718600 | tf_op jit(solution)/shard_map/ppermute | solution.py:547
  30.7 58.8 %collective-permute-start.11 = (bf16[128,5120]{1,0:T(8,128)(2,1)}, bf16[128,5120]{1,0:T(8,128)(2,1)}, u32[]{:S(2)}, u32[]{:S(2)}) collective-permute-start(bf16[128,5120]{1,0:T(8,128)(2,1)} %cut.3.refs_2_), channel_id=1, source_target_pairs={{0,2},{1,3},{2,0},{3,1},{4,6},{5,7},{6,4},{7,5},{8,10},{9,11},{10,... | collective-permute-start | bytes 3932168 | tf_op jit(solution)/shard_map/ppermute | solution.py:547
  39.4 88.1 %collective-permute-start.15 = (bf16[256,1024]{1,0:T(8,128)(2,1)}, bf16[256,1024]{1,0:T(8,128)(2,1)}, u32[]{:S(2)}, u32[]{:S(2)}) collective-permute-start(bf16[256,1024]{1,0:T(8,128)(2,1)} %pick.5.refs_2_), channel_id=1, source_target_pairs={{0,2},{1,3},{2,0},{3,1},{4,6},{5,7},{6,4},{7,5},{8,10},{9,11},{10,... | collective-permute-start | bytes 1572872 | tf_op jit(solution)/shard_map/ppermute | solution.py:547
  127.3 67.0 %collective-permute-start.16 = (bf16[512,1536]{1,0:T(8,128)(2,1)}, bf16[512,1536]{1,0:T(8,128)(2,1)}, u32[]{:S(2)}, u32[]{:S(2)}) collective-permute-start(bf16[512,1536]{1,0:T(8,128)(2,1)} %get-tuple-element.122), channel_id=1, source_target_pairs={{0,1},{1,0},{2,3},{3,2},{4,5},{5,4},{6,7},{7,6},{8,9},{9,8},{10,11... | collective-permute-start | bytes 4718600 | tf_op jit(solution)/shard_map/ppermute | solution.py:547
  192.7 54.5 %collective-permute-start.26 = (bf16[1024,1024]{1,0:T(8,128)(2,1)}, bf16[1024,1024]{1,0:T(8,128)(2,1)}, u32[]{:S(2)}, u32[]{:S(2)}) collective-permute-start(bf16[1024,1024]{1,0:T(8,128)(2,1)} %grad_x.3.refs_5_), channel_id=1, source_target_pairs={{0,2},{1,3},{2,0},{3,1},{4,6},{5,7},{6,4},{7,5},{8,10},{9,11},{10,... | collective-permute-start | bytes 6291464 | tf_op jit(solution)/shard_map/ppermute | solution.py:547
  202.2 89.6 %collective-permute-start.30 = (bf16[1024,1024]{1,0:T(8,128)(2,1)}, bf16[1024,1024]{1,0:T(8,128)(2,1)}, u32[]{:S(2)}, u32[]{:S(2)}) collective-permute-start(bf16[1024,1024]{1,0:T(8,128)(2,1)} %grad_x.4.refs_10_), channel_id=1, source_target_pairs={{0,2},{1,3},{2,0},{3,1},{4,6},{5,7},{6,4},{7,5},{8,10},{9,11},{10,... | collective-permute-start | bytes 6291464 | tf_op jit(solution)/shard_map/ppermute | solution.py:547
  226.4 32.9 %collective-permute-start.23 = (bf16[512,1024]{1,0:T(8,128)(2,1)}, bf16[512,1024]{1,0:T(8,128)(2,1)}, u32[]{:S(2)}, u32[]{:S(2)}) collective-permute-start(bf16[512,1024]{1,0:T(8,128)(2,1)} %get-tuple-element.130.refs_1_.refs_9_), channel_id=1, source_target_pairs={{0,1},{1,0},{2,3},{3,2},{4,5},{5,4},{6,7},{7,6},{8,9},{9,8},{10,11... | collective-permute-start | bytes 3145736 | tf_op jit(solution)/shard_map/ppermute | solution.py:547
  258.3 25.5 %collective-permute-start.28 = (bf16[512,1024]{1,0:T(8,128)(2,1)}, bf16[512,1024]{1,0:T(8,128)(2,1)}, u32[]{:S(2)}, u32[]{:S(2)}) collective-permute-start(bf16[512,1024]{1,0:T(8,128)(2,1)} %get-tuple-element.140), channel_id=1, source_target_pairs={{0,4},{4,0},{8,12},{12,8},{16,20},{20,16},{24,28},{28,24},{1,5},{5... | collective-permute-start | bytes 3145736 | tf_op jit(solution)/shard_map/ppermute | solution.py:547
  268.7 62.6 %collective-permute-start.27 = (bf16[1024,1024]{1,0:T(8,128)(2,1)}, bf16[1024,1024]{1,0:T(8,128)(2,1)}, u32[]{:S(2)}, u32[]{:S(2)}) collective-permute-start(bf16[1024,1024]{1,0:T(8,128)(2,1)} %grad_x.5.refs_6_), channel_id=1, source_target_pairs={{0,2},{1,3},{2,0},{3,1},{4,6},{5,7},{6,4},{7,5},{8,10},{9,11},{10,... | collective-permute-start | bytes 6291464 | tf_op jit(solution)/shard_map/ppermute | solution.py:547
  290.3 65.0 %collective-permute-start.36 = (f32[32,1024]{1,0:T(8,128)}, f32[32,1024]{1,0:T(8,128)}, u32[]{:S(2)}, u32[]{:S(2)}) collective-permute-start(f32[32,1024]{1,0:T(8,128)} %lines_add.5.refs_6_.refs_1_), channel_id=1, source_target_pairs={{0,2},{1,3},{2,0},{3,1},{4,6},{5,7},{6,4},{7,5},{8,10},{9,11},{10,... | collective-permute-start | bytes 393224 | tf_op jit(solution)/shard_map/ppermute | solution.py:547
  299.3 24.1 %collective-permute-start.33 = (bf16[512,1024]{1,0:T(8,128)(2,1)}, bf16[512,1024]{1,0:T(8,128)(2,1)}, u32[]{:S(2)}, u32[]{:S(2)}) collective-permute-start(bf16[512,1024]{1,0:T(8,128)(2,1)} %get-tuple-element.147), channel_id=1, source_target_pairs={{0,4},{4,0},{8,12},{12,8},{16,20},{20,16},{24,28},{28,24},{1,5},{5... | collective-permute-start | bytes 3145736 | tf_op jit(solution)/shard_map/ppermute | solution.py:547
  302.6 24.8 %collective-permute-start.32 = (bf16[256,1024]{1,0:T(8,128)(2,1)}, bf16[256,1024]{1,0:T(8,128)(2,1)}, u32[]{:S(2)}, u32[]{:S(2)}) collective-permute-start(bf16[256,1024]{1,0:T(8,128)(2,1)} %grad_add.8.refs_5_.refs_1_), channel_id=1, source_target_pairs={{0,16},{4,20},{8,24},{12,28},{16,0},{20,4},{24,8},{28,12},{1,17},{... | collective-permute-start | bytes 1572872 | tf_op jit(solution)/shard_map/ppermute | solution.py:547
  336.6 23.3 %collective-permute-start.35 = (bf16[256,1024]{1,0:T(8,128)(2,1)}, bf16[256,1024]{1,0:T(8,128)(2,1)}, u32[]{:S(2)}, u32[]{:S(2)}) collective-permute-start(bf16[256,1024]{1,0:T(8,128)(2,1)} %get-tuple-element.152), channel_id=1, source_target_pairs={{0,4},{4,0},{8,12},{12,8},{16,20},{20,16},{24,28},{28,24},{1,5},{5... | collective-permute-start | bytes 1572872 | tf_op jit(solution)/shard_map/ppermute | solution.py:547
  346.5 24.9 %collective-permute-start.42 = (bf16[256,1024]{1,0:T(8,128)(2,1)}, bf16[256,1024]{1,0:T(8,128)(2,1)}, u32[]{:S(2)}, u32[]{:S(2)}) collective-permute-start(bf16[256,1024]{1,0:T(8,128)(2,1)} %grad_add.10.refs_3_.refs_1_), channel_id=1, source_target_pairs={{0,16},{4,20},{8,24},{12,28},{16,0},{20,4},{24,8},{28,12},{1,17},{... | collective-permute-start | bytes 1572872 | tf_op jit(solution)/shard_map/ppermute | solution.py:547
  354.4 36.8 %collective-permute-start.46 = (bf16[512,1024]{1,0:T(8,128)(2,1)}, bf16[512,1024]{1,0:T(8,128)(2,1)}, u32[]{:S(2)}, u32[]{:S(2)}) collective-permute-start(bf16[512,1024]{1,0:T(8,128)(2,1)} %grad_join.4.refs_3_.refs_1_), channel_id=1, source_target_pairs={{0,4},{4,0},{8,12},{12,8},{16,20},{20,16},{24,28},{28,24},{1,5},{5... | collective-permute-start | bytes 3145736 | tf_op jit(solution)/shard_map/ppermute | solution.py:547
  357.4 28.7 %collective-permute-start.47 = (f32[32,1024]{1,0:T(8,128)}, f32[32,1024]{1,0:T(8,128)}, u32[]{:S(2)}, u32[]{:S(2)}) collective-permute-start(f32[32,1024]{1,0:T(8,128)} %lines_add.6.refs_5_.refs_1_), channel_id=1, source_target_pairs={{0,4},{4,0},{8,12},{12,8},{16,20},{20,16},{24,28},{28,24},{1,5},{5... | collective-permute-start | bytes 393224 | tf_op jit(solution)/shard_map/ppermute | solution.py:547
  371.4 43.7 %collective-permute-start.39 = (bf16[256,1024]{1,0:T(8,128)(2,1)}, bf16[256,1024]{1,0:T(8,128)(2,1)}, u32[]{:S(2)}, u32[]{:S(2)}) collective-permute-start(bf16[256,1024]{1,0:T(8,128)(2,1)} %relay.2.refs_3_), channel_id=1, source_target_pairs={{0,2},{1,3},{2,0},{3,1},{4,6},{5,7},{6,4},{7,5},{8,10},{9,11},{10,... | collective-permute-start | bytes 1572872 | tf_op jit(solution)/shard_map/ppermute | solution.py:547
  377.1 23.6 %collective-permute-start.45 = (bf16[256,1024]{1,0:T(8,128)(2,1)}, bf16[256,1024]{1,0:T(8,128)(2,1)}, u32[]{:S(2)}, u32[]{:S(2)}) collective-permute-start(bf16[256,1024]{1,0:T(8,128)(2,1)} %grad_add.11.refs_3_.refs_1_), channel_id=1, source_target_pairs={{0,8},{4,12},{8,0},{12,4},{16,24},{20,28},{24,16},{28,20},{1,9},{5... | collective-permute-start | bytes 1572872 | tf_op jit(solution)/shard_map/ppermute | solution.py:547
  382.7 24.3 %collective-permute-start.44 = (bf16[128,1024]{1,0:T(8,128)(2,1)}, bf16[128,1024]{1,0:T(8,128)(2,1)}, u32[]{:S(2)}, u32[]{:S(2)}) collective-permute-start(bf16[128,1024]{1,0:T(8,128)(2,1)} %grad_add.12.refs_3_.refs_1_), channel_id=1, source_target_pairs={{0,16},{4,20},{8,24},{12,28},{16,0},{20,4},{24,8},{28,12},{1,17},{... | collective-permute-start | bytes 786440 | tf_op jit(solution)/shard_map/ppermute | solution.py:547
  391.2 36.1 %collective-permute-start.50 = (f32[32,1024]{1,0:T(8,128)}, f32[32,1024]{1,0:T(8,128)}, u32[]{:S(2)}, u32[]{:S(2)}) collective-permute-start(f32[32,1024]{1,0:T(8,128)} %lines_add.7.refs_3_.refs_1_), channel_id=1, source_target_pairs={{0,8},{4,12},{8,0},{12,4},{16,24},{20,28},{24,16},{28,20},{1,9},{5... | collective-permute-start | bytes 393224 | tf_op jit(solution)/shard_map/ppermute | solution.py:547
  405.7 26.0 %collective-permute-start.49 = (bf16[512,1024]{1,0:T(8,128)(2,1)}, bf16[512,1024]{1,0:T(8,128)(2,1)}, u32[]{:S(2)}, u32[]{:S(2)}) collective-permute-start(bf16[512,1024]{1,0:T(8,128)(2,1)} %grad_join.5.refs_3_.refs_1_), channel_id=1, source_target_pairs={{0,4},{4,0},{8,12},{12,8},{16,20},{20,16},{24,28},{28,24},{1,5},{5... | collective-permute-start | bytes 3145736 | tf_op jit(solution)/shard_map/ppermute | solution.py:547
  426.2 24.0 %collective-permute-start.55 = (bf16[256,1024]{1,0:T(8,128)(2,1)}, bf16[256,1024]{1,0:T(8,128)(2,1)}, u32[]{:S(2)}, u32[]{:S(2)}) collective-permute-start(bf16[256,1024]{1,0:T(8,128)(2,1)} %grad_join.7.refs_3_.refs_1_), channel_id=1, source_target_pairs={{0,4},{4,0},{8,12},{12,8},{16,20},{20,16},{24,28},{28,24},{1,5},{5... | collective-permute-start | bytes 1572872 | tf_op jit(solution)/shard_map/ppermute | solution.py:547
  (72 other events, 676.7 us)
Sparse Core Ops, SparseCore 0:
  54.4 76.7 all-gather.1
